TPU v7x, 256 devices: a whole 4x4x8 slice. The times are simulated.
256 devices in a mesh: path: 64 (over y_lo, x, z), shard: 4 (over y_hi, core).
Axes of the slice: x: 4, y: 4 (y_hi: 2, y_lo: 2; y = y_hi * 2 + y_lo), z: 8, core: 2. Of those that a mesh axis runs over, the one named last changes fastest.
Arguments:
- params: float32 [64, 2, 256, 2048], P('path', None, 'shard'), may hold values from -6 to 6
- grads: bfloat16 [64, 2, 256, 2048], P('path', None, 'shard'), may hold values from -480 to 480
- adam_mean: float32 [64, 2, 256, 2048], P('path', None, 'shard'), may hold values from -1.2 to 1.2
- adam_square: float32 [64, 2, 256, 2048], P('path', None, 'shard'), may hold values from 0.001 to 0.3
- anchor: float32 [28, 256, 2048], P(None, ('shard', 'path')), may hold values from -6 to 6
- momentum: float32 [28, 256, 2048], P(None, ('shard', 'path')), may hold values from -3 to 3
- module_low: int32 [64], replicated, may hold values from 0 to 11
- module_high: int32 [64], replicated, may hold values from 0 to 15
- tok_counts: int32 [64], replicated, may hold values from 1024 to 8191
Outputs:
- new_params: float32 [64, 2, 256, 2048], P('path', None, 'shard')
- new_mean: float32 [64, 2, 256, 2048], P('path', None, 'shard')
- new_square: float32 [64, 2, 256, 2048], P('path', None, 'shard')
- new_anchor: float32 [28, 256, 2048], P(None, ('shard', 'path'))
- new_moment: float32 [28, 256, 2048], P(None, ('shard', 'path'))
All inputs are finite; a program needn't handle non-finite values.
Results may differ from a plain program's by a relative error of at most 0.0004.
Values sent between devices are 32-bit elements; how exact they have to be, the bound alone decides.
No kernel may reach another device: no remote copies, remote signals or barrier semaphores. Data moves between devices by JAX's collectives and lax.ppermute only.
A program may use at most 128 MiB of HBM per device.

v0:
```python
import math

import jax
import jax.numpy as jnp
from jax import lax
from jax.sharding import PartitionSpec as P

LOW = 12
INNER_STEP = 500


BETA_FIRST = 0.9
BETA_SECOND = 0.95
LEARN_RATE = 0.0004
WEIGHT_DECAY = 0.1
ADAM_EPS = 1e-08
OUTER_RATE = 0.7
OUTER_MOMENTUM = 0.9
CLIP_SHARE = 0.2


def shards(
    params, grads, adam_mean, adam_square, anchor, momentum, module_low, module_high, tok_counts
):
    gradient = grads.astype(jnp.float32)
    local_squares = jnp.sum(gradient * gradient)
    squares = lax.psum(local_squares, "shard")
    all_rows = params.shape[2] * lax.axis_size("shard")
    clip_norm = CLIP_SHARE * math.sqrt(2 * all_rows * params.shape[3])
    factor = jnp.minimum(1.0, clip_norm / jnp.sqrt(squares + 1e-06))
    clipped = gradient * factor
    new_mean = BETA_FIRST * adam_mean + (1.0 - BETA_FIRST) * clipped
    new_square = BETA_SECOND * adam_square + (1.0 - BETA_SECOND) * clipped * clipped
    first_fix = 1.0 - BETA_FIRST**INNER_STEP
    second_fix = 1.0 - BETA_SECOND**INNER_STEP
    update = (
        new_mean / first_fix / (jnp.sqrt(new_square / second_fix) + ADAM_EPS)
        + WEIGHT_DECAY * params
    )
    stepped = params - LEARN_RATE * update
    path_index = lax.axis_index("path")
    module_count = anchor.shape[0]
    module_ids = jnp.stack([module_low, module_high + LOW], axis=1)
    onehot = (
        module_ids[None, :, :] == jnp.arange(module_count, dtype=jnp.int32)[:, None, None]
    ).astype(jnp.float32)
    weights = onehot * tok_counts.astype(jnp.float32)[None, :, None]
    totals = jnp.sum(weights, axis=(1, 2))
    own_weights = lax.dynamic_index_in_dim(weights, path_index, axis=1, keepdims=False)
    partial_terms = jnp.einsum(
        "ml,lrd->mrd", own_weights, stepped[0], precision=lax.Precision.HIGHEST
    )
    summed = lax.psum_scatter(partial_terms, "path", scatter_dimension=1, tiled=True)
    outer_grad = (totals[:, None, None] * anchor - summed) / jnp.maximum(totals, 1.0)[:, None, None]
    new_moment = OUTER_MOMENTUM * momentum + outer_grad
    new_anchor = anchor - OUTER_RATE * (outer_grad + OUTER_MOMENTUM * new_moment)
    own_ids = lax.dynamic_index_in_dim(module_ids, path_index, axis=0, keepdims=False)
    returned = jnp.take(lax.all_gather(new_anchor, "path", axis=1, tiled=True), own_ids, axis=0)
    new_params = returned[None]
    return (new_params, new_mean, new_square, new_anchor, new_moment)


def solution(mesh):
    return jax.shard_map(
        shards,
        mesh=mesh,
        in_specs=(
            P("path", None, "shard", None),
            P("path", None, "shard", None),
            P("path", None, "shard", None),
            P("path", None, "shard", None),
            P(None, ("shard", "path"), None),
            P(None, ("shard", "path"), None),
            P(),
            P(),
            P(),
        ),
        out_specs=(
            P("path", None, "shard", None),
            P("path", None, "shard", None),
            P("path", None, "shard", None),
            P(None, ("shard", "path"), None),
            P(None, ("shard", "path"), None),
        ),
        check_vma=False,
    )
```

profile of v0, /device:TPU:8, one launch (start us, length us, event | category | flops | bytes accessed | tf_op | source)
XLA Modules:
  0.0 759.4 jit_solution(5562118132684493279)
XLA Ops:
  7.2 0.0 reduce-scatter.2.cloned.1.call-start
  7.2 1.9 fusion.2
  9.1 9.8 %psum.7 = f32[]{:T(128)} all-reduce(f32[]{:T(128)} %fusion.2), channel_id=1, replica_groups=mesh['path'=64,'shard'=4] {'shard'}, use_global_device_ids=true, to_apply=%region_2.0 | all-reduce | flops 1 | bytes 8 | tf_op jit(solution)/shard_map/psum | solution.py:27
  19.6 0.7 add_bitcast_fusion
  20.3 0.7 convert_element_type.7
  20.9 0.7 pad_add_fusion
  21.6 0.1 copy.30
  21.7 0.2 compare_select_fusion
  21.9 4.1 subtract_bitcast_fusion
  26.0 0.0 copy-start
  26.0 0.0 copy-start.1
  26.0 16.0 %fusion.4 = f32[28,64,2048]{2,0,1:T(8,128)} fusion(f32[2,64,2048]{2,1,0:T(8,128)S(1)} %get-tuple-element.20, f32[28,64,2]{0,2,1:T(2,128)S(1)} %get-tuple-element.25, s32[]{:T(128)S(6)} %select_n.33), kind=kOutput, calls=%fused_computation.9 | convolution fusion | flops 88080384 | bytes 15729668 | tf_op jit(solution)/shard_map/ml,lrd->mrd/dot_general | solution.py:50
  42.0 0.0 reduce-scatter.2.cloned.1.call-update
  42.1 0.2 all-gather.2.cloned.1.call-start
  42.3 354.5 %reduce-scatter.2.cloned.1.call-done = f32[28,1,2048]{2,0,1:T(8,128)} async-done(((f32[28,64,2048]{2,0,1:T(8,128)}), f32[28,1,2048]{2,0,1:T(8,128)}) %reduce-scatter.2.cloned.1.call-update) | async-done | bytes 229392 | tf_op jit(solution)/shard_map/reduce_scatter | solution.py:53
  396.9 0.0 copy-done
  396.9 0.0 copy-done.1
  396.9 1.9 fusion.8
  398.7 0.0 all-gather.2.cloned.1.call-update
  398.7 0.2 dynamic-slice_reduce_fusion
  399.0 1.9 copy.36
  400.8 0.9 copy.37
  401.8 324.4 %all-gather.2.cloned.1.call-done = f32[28,64,2048]{2,0,1:T(8,128)} async-done(((f32[28,1,2048]{2,0,1:T(8,128)}), f32[28,64,2048]{2,0,1:T(8,128)}) %all-gather.2.cloned.1.call-update) | async-done | bytes 14680080 | tf_op jit(solution)/shard_map/all_gather | solution.py:58
  726.1 19.5 %copy.35 = f32[28,64,2048]{2,1,0:T(8,128)} copy(f32[28,64,2048]{2,0,1:T(8,128)} %all-gather.2.cloned.1.call-done) | data formatting | bytes 29360128 | tf_op jit(solution)/shard_map/all_gather | solution.py:58
  745.6 5.8 gather_fusion
  751.4 1.1 bitcast_select_fusion
  (4 shorter events, 0.0 us)
Async XLA Ops:
  7.2 389.7 %reduce-scatter.2.cloned.1.call-start = ((), (), s32[]{:S(2)}) async-start(), calls=%async_computation.1 | async-start | bytes 17039360 | tf_op jit(solution)/shard_map/reduce_scatter | solution.py:53
  26.0 370.8 %copy-start = (f32[28,1,2048]{2,1,0:T(1,128)S(1)}, f32[28,1,2048]{2,1,0:T(1,128)}, u32[]{:S(2)}) copy-start(f32[28,1,2048]{2,1,0:T(1,128)} %param.14) | copy-start | bytes 688132
  26.0 370.8 %copy-start.1 = (f32[28,1,2048]{2,1,0:T(1,128)S(1)}, f32[28,1,2048]{2,1,0:T(1,128)}, u32[]{:S(2)}) copy-start(f32[28,1,2048]{2,1,0:T(1,128)} %param.13) | copy-start | bytes 688132
  42.1 684.1 %all-gather.2.cloned.1.call-start = ((), (), s32[]{:S(2)}) async-start(), calls=%async_computation.2 | async-start | bytes 17039360 | tf_op jit(solution)/shard_map/all_gather | solution.py:58
Sparse Core Ops, SparseCore 0:
  42.2 354.6 reduce-scatter.1
  399.2 326.8 all-gather.1
where the time goes:
time: 760 us; the launch traced here: 759 us
  waiting for transfers between devices  679 us (89%)
  local copies, waits for them, and re-layouts  28.4 us (4%)
  matrix products  16 us (2%)
  between operations  14.8 us (2%)
  other arithmetic  11.3 us (1%)
  blocking collectives  9.8 us (1%)
    reduce_scatter x1, waiting for transfers between devices, shards(): lax.psum_scatter(partial_terms, 'path', scatter_dimension=1, tiled=True)  355 us
    all_gather x1, waiting for transfers between devices, shards(): lax.all_gather(new_anchor, 'path', axis=1, tiled=True)  324 us
    all_gather x1, local copies, waits for them, and re-layouts, shards(): lax.all_gather(new_anchor, 'path', axis=1, tiled=True)  19.5 us
    dot_general x1, matrix products, shards(): jnp.einsum('ml,lrd->mrd', own_weights, stepped[0], precision=lax.Precisio...  16 us
  transfers between devices with their start and end apart: 2, of which 2 were waited for; matrix products, arithmetic and copies ran while one was open for 0% of the time, Pallas kernels for 0%

commit v1 on v0

v1 whole, which is shorter than its diff:
```python
import math

import jax
import jax.numpy as jnp
from jax import lax
from jax.experimental import pallas as pl
from jax.experimental.pallas import tpu as pltpu
from jax.sharding import PartitionSpec as P

LOW = 12
INNER_STEP = 500


BETA_FIRST = 0.9
BETA_SECOND = 0.95
LEARN_RATE = 0.0004
WEIGHT_DECAY = 0.1
ADAM_EPS = 1e-08
OUTER_RATE = 0.7
OUTER_MOMENTUM = 0.9
CLIP_SHARE = 0.2

LANES = 128
FIRST_FIX = 1.0 - BETA_FIRST**INNER_STEP
SECOND_FIX = 1.0 - BETA_SECOND**INNER_STEP


def inner_kernel(scalars, params, grads, mean, square, new_mean, new_square, send):
    factor = scalars[0]
    tokens = scalars[1]
    levels, rows, width = params.shape
    chunks = width // LANES
    for level in range(levels):
        for row in range(0, rows, 16):
            for chunk in range(chunks):
                lanes = slice(chunk * LANES, (chunk + 1) * LANES)
                at = (level, slice(row, row + 16), lanes)
                clipped = grads[at].astype(jnp.float32) * factor
                first = BETA_FIRST * mean[at] + (1.0 - BETA_FIRST) * clipped
                second = BETA_SECOND * square[at] + (1.0 - BETA_SECOND) * clipped * clipped
                new_mean[at] = first
                new_square[at] = second
                fixed = second * (1.0 / SECOND_FIX)
                root = fixed * lax.rsqrt(fixed) + ADAM_EPS
                old = params[at]
                update = first * (1.0 / FIRST_FIX) * pl.reciprocal(root, approx=True) + WEIGHT_DECAY * old
                stepped = old - LEARN_RATE * update
                send[slice(row, row + 16), level * chunks + chunk, :] = stepped * tokens


def outer_kernel(low, high, tokens, received, anchor, momentum, new_anchor, new_moment, send, summed, totals):
    paths = received.shape[0]
    modules, chunks, _ = anchor.shape
    summed[...] = jnp.zeros_like(summed)
    for module in range(modules):
        totals[module] = 0

    def add(path, carry):
        for level in range(2):
            module = low[path] if level == 0 else high[path] + LOW
            summed[module] += received[path, level * chunks : (level + 1) * chunks, :]
            totals[module] += tokens[path]
        return carry

    lax.fori_loop(0, paths, add, 0, unroll=4)
    for module in range(modules):
        total = jnp.full((chunks, LANES), totals[module], jnp.int32).astype(jnp.float32)
        old = anchor[module]
        outer_grad = (total * old - summed[module]) / jnp.maximum(total, 1.0)
        moment = OUTER_MOMENTUM * momentum[module] + outer_grad
        new_moment[module] = moment
        new_anchor[module] = old - OUTER_RATE * (outer_grad + OUTER_MOMENTUM * moment)

    def pick(path, carry):
        for level in range(2):
            module = low[path] if level == 0 else high[path] + LOW
            send[path, level * chunks : (level + 1) * chunks, :] = new_anchor[module]
        return carry

    lax.fori_loop(0, paths, pick, 0, unroll=4)


def place_kernel(received, new_params):
    levels, rows, width = new_params.shape
    chunks = width // LANES
    for level in range(levels):
        for row in range(0, rows, 8):
            for chunk in range(chunks):
                lanes = slice(chunk * LANES, (chunk + 1) * LANES)
                new_params[level, slice(row, row + 8), lanes] = received[slice(row, row + 8), level * chunks + chunk, :]


VMEM = pl.BlockSpec(memory_space=pltpu.VMEM)
SMEM = pl.BlockSpec(memory_space=pltpu.SMEM)


def shards(
    params, grads, adam_mean, adam_square, anchor, momentum, module_low, module_high, tok_counts
):
    _, levels, rows, width = params.shape
    modules = anchor.shape[0]
    paths = module_low.shape[0]
    chunks = width // LANES
    f32 = jnp.float32
    gradient = grads.astype(f32)
    squares = lax.psum(jnp.sum(gradient * gradient), "shard")
    all_rows = rows * lax.axis_size("shard")
    clip_norm = CLIP_SHARE * math.sqrt(2 * all_rows * width)
    factor = jnp.minimum(1.0, clip_norm / jnp.sqrt(squares + 1e-06))
    own_tokens = lax.dynamic_index_in_dim(tok_counts, lax.axis_index("path"), keepdims=False)
    scalars = jnp.stack([factor, own_tokens.astype(f32)])
    local = jax.ShapeDtypeStruct((levels, rows, width), f32)
    wire = jax.ShapeDtypeStruct((rows, levels * chunks, LANES), f32)
    owned = jax.ShapeDtypeStruct((modules, chunks, LANES), f32)
    new_mean, new_square, send = pl.pallas_call(
        inner_kernel,
        out_shape=(local, local, wire),
        in_specs=[SMEM] + [VMEM] * 4,
        out_specs=(VMEM,) * 3,
        compiler_params=pltpu.CompilerParams(vmem_limit_bytes=16 * 1024 * 1024),
        name="inner",
    )(scalars, params[0], grads[0], adam_mean[0], adam_square[0])
    received = lax.all_to_all(send, "path", 0, 0, tiled=True)
    new_anchor, new_moment, send_back = pl.pallas_call(
        outer_kernel,
        out_shape=(owned, owned, jax.ShapeDtypeStruct((paths, levels * chunks, LANES), f32)),
        in_specs=[SMEM] * 3 + [VMEM] * 3,
        out_specs=(VMEM,) * 3,
        scratch_shapes=[pltpu.VMEM((modules, chunks, LANES), f32), pltpu.SMEM((modules,), jnp.int32)],
        compiler_params=pltpu.CompilerParams(vmem_limit_bytes=16 * 1024 * 1024),
        name="outer",
    )(
        module_low, module_high, tok_counts, received,
        anchor.reshape(modules, chunks, LANES), momentum.reshape(modules, chunks, LANES),
    )
    returned = lax.all_to_all(send_back, "path", 0, 0, tiled=True)
    new_params = pl.pallas_call(
        place_kernel,
        out_shape=local,
        in_specs=[VMEM],
        out_specs=VMEM,
        compiler_params=pltpu.CompilerParams(vmem_limit_bytes=16 * 1024 * 1024),
        name="place",
    )(returned)
    return (
        new_params[None], new_mean[None], new_square[None],
        new_anchor.reshape(anchor.shape), new_moment.reshape(anchor.shape),
    )


def solution(mesh):
    return jax.shard_map(
        shards,
        mesh=mesh,
        in_specs=(
            P("path", None, "shard", None),
            P("path", None, "shard", None),
            P("path", None, "shard", None),
            P("path", None, "shard", None),
            P(None, ("shard", "path"), None),
            P(None, ("shard", "path"), None),
            P(),
            P(),
            P(),
        ),
        out_specs=(
            P("path", None, "shard", None),
            P("path", None, "shard", None),
            P("path", None, "shard", None),
            P(None, ("shard", "path"), None),
            P(None, ("shard", "path"), None),
        ),
        check_vma=False,
    )
```

time: 760 us -> 99.7 us (0.13)
  waiting for transfers between devices: 679 us -> 0 us
  blocking collectives: 9.8 us -> 82.7 us
  local copies, waits for them, and re-layouts: 28.4 us -> 5.58 us
  matrix products: 16 us -> 0 us
  between operations: 14.8 us -> 2 us
  other arithmetic: 11.3 us -> 2.05 us
    reduce_scatter x1 -> x0, waiting for transfers between devices: 355 us -> none  [shards(): lax.psum_scatter(partial_terms, 'path', scatter_dimension=1, tiled=True)]
    all_gather x1 -> x0, waiting for transfers between devices: 324 us -> none  [shards(): lax.all_gather(new_anchor, 'path', axis=1, tiled=True)]
    all_to_all x0 -> x2, blocking collectives: none -> 72.8 us  [the longest x1 40.6 us: shards(): received = lax.all_to_all(send, 'path', 0, 0, tiled=True)]
    all_gather x1 -> x0, local copies, waits for them, and re-layouts: 19.5 us -> none  [shards(): lax.all_gather(new_anchor, 'path', axis=1, tiled=True)]
    dot_general x1 -> x0, matrix products: 16 us -> none  [shards(): jnp.einsum('ml,lrd->mrd', own_weights, stepped[0], precision=lax.Precisio...]
  transfers between devices with their start and end apart: 2 -> 0, of which waited for: 2 -> 0; matrix products, arithmetic and copies ran while one was open for 0% -> 0% of each run, Pallas kernels for 0% -> 0%
where the time goes in v1:
time: 99.7 us; the launch traced here: 98.6 us
  blocking collectives  82.7 us (83%)
  Pallas kernels  6.25 us (6%)
  local copies, waits for them, and re-layouts  5.58 us (6%)
  other arithmetic  2.05 us (2%)
  between operations  2 us (2%)
    all_to_all x1, blocking collectives, shards(): received = lax.all_to_all(send, 'path', 0, 0, tiled=True)  40.6 us
    all_to_all x1, blocking collectives, shards(): returned = lax.all_to_all(send_back, 'path', 0, 0, tiled=True)  32.2 us
    psum x1, blocking collectives, shards(): squares = lax.psum(jnp.sum(gradient * gradient), 'shard')  9.84 us
    unnamed x18, local copies, waits for them, and re-layouts  5 us
    pallas_call x1, Pallas kernels, shards(): pl.pallas_call(inner_kernel, out_shape=(local, local, wire), in_specs=[SM...  2.42 us
    pallas_call x1, Pallas kernels, shards(): pl.pallas_call(outer_kernel, out_shape=(owned, owned, jax.ShapeDtypeStruc...  2.29 us

profile of v1, /device:TPU:8, one launch (start us, length us, event | category | flops | bytes accessed | tf_op | source)
XLA Modules:
  0.0 98.6 jit_solution(13259071838993721206)
XLA Ops:
  0.6 0.0 copy-start
  0.6 2.0 %multiply_reduce_fusion = f32[]{:T(128)} fusion(bf16[1,2,64,2048]{3,2,1,0:T(8,128)(2,1)} %param.10), kind=kLoop, calls=%fused_computation | loop fusion | flops 786431 | bytes 524292 | tf_op jit(solution)/shard_map/reduce_sum | solution.py:106
  2.6 0.0 copy-start.8
  2.6 0.7 copy-done.8
  3.3 0.6 dynamic_slice.4
  4.5 9.8 %psum.7 = f32[]{:T(128)} all-reduce(f32[]{:T(128)} %multiply_reduce_fusion), channel_id=1, replica_groups=mesh['path'=64,'shard'=4] {'shard'}, use_global_device_ids=true, to_apply=%region_1.0 | all-reduce | flops 1 | bytes 8 | tf_op jit(solution)/shard_map/psum | solution.py:106
  15.0 0.1 pad_maximum_fusion.scalars
  15.1 0.0 copy-done
  15.1 0.0 copy-start.1
  15.1 1.2 %copy-done.1 = f32[1,2,64,2048]{3,2,1,0:T(8,128)S(1)} copy-done((f32[1,2,64,2048]{3,2,1,0:T(8,128)S(1)}, f32[1,2,64,2048]{3,2,1,0:T(8,128)}, u32[]{:S(2)}) %copy-start.1) | copy-done | bytes 1048600
  16.4 0.0 copy-start.2
  16.4 1.2 %copy-done.2 = f32[1,2,64,2048]{3,2,1,0:T(8,128)S(1)} copy-done((f32[1,2,64,2048]{3,2,1,0:T(8,128)S(1)}, f32[1,2,64,2048]{3,2,1,0:T(8,128)}, u32[]{:S(2)}) %copy-start.2) | copy-done | bytes 1048600
  17.6 0.0 copy-start.3
  17.6 1.2 %copy-done.3 = f32[1,2,64,2048]{3,2,1,0:T(8,128)S(1)} copy-done((f32[1,2,64,2048]{3,2,1,0:T(8,128)S(1)}, f32[1,2,64,2048]{3,2,1,0:T(8,128)}, u32[]{:S(2)}) %copy-start.3) | copy-done | bytes 1048600
  18.8 2.4 %inner.1 = (f32[2,64,2048]{2,1,0:T(8,128)}, f32[2,64,2048]{2,1,0:T(8,128)}, f32[64,32,128]{2,1,0:T(8,128)S(1)}) custom-call(f32[2]{0:T(128)S(1)} %pad_maximum_fusion.scalars, f32[2,64,2048]{2,1,0:T(8,128)S(1)} %bitcast.13, bf16[2,64,2048]{2,1,0:T(8,128)(2,1)S(1)} %bitcast.12, f32[2,64,2048]{2,1,0:T(8,128)S(1)} %bitcast.14, f32[2,64,2048]{2,1,0:T(8,128)S(1)} %bitcast.15), custom_call_target="tpu_custom_call" | custom-call | tf_op jit(solution)/shard_map/inner/pallas_call | solution.py:115
  21.2 0.0 copy-start.4
  21.2 0.0 copy-start.5
  21.2 40.6 %all_to_all.10.received = f32[64,32,128]{2,1,0:T(8,128)S(1)} all-to-all(f32[64,32,128]{2,1,0:T(8,128)S(1)} %get-tuple-element.11), channel_id=1, replica_groups=mesh['path'=64,'shard'=4] {'path'}, dimensions={0} | all-to-all | bytes 2097152 | tf_op jit(solution)/shard_map/all_to_all | solution.py:123
  61.9 0.0 copy-start.6
  61.9 0.0 copy-start.7
  61.9 0.0 copy-done.4
  61.9 0.0 copy-done.5
  61.9 0.6 copy-done.6
  62.5 0.0 copy-done.7
  62.5 2.3 %outer.1 = (f32[28,16,128]{2,1,0:T(8,128)}, f32[28,16,128]{2,1,0:T(8,128)}, f32[64,32,128]{2,1,0:T(8,128)S(1)}) custom-call(s32[64]{0:T(128)S(1)} %copy-done.6, s32[64]{0:T(128)S(1)} %copy-done.7, s32[64]{0:T(128)S(1)} %copy-done.8, f32[64,32,128]{2,1,0:T(8,128)S(1)} %all_to_all.10.received, f32[28,16,128]{2,1,0:T(8,128)S(1)} %bitcast.16, ...), custom_call_target="tpu_custom_call" | custom-call | tf_op jit(solution)/shard_map/outer/pallas_call | solution.py:124
  64.8 32.2 %all_to_all.11.received = f32[64,32,128]{2,1,0:T(8,128)S(1)} all-to-all(f32[64,32,128]{2,1,0:T(8,128)S(1)} %get-tuple-element.12), channel_id=1, replica_groups=mesh['path'=64,'shard'=4] {'path'}, dimensions={0} | all-to-all | bytes 2097152 | tf_op jit(solution)/shard_map/all_to_all | solution.py:136
  97.0 1.5 %place.1 = f32[2,64,2048]{2,1,0:T(8,128)} custom-call(f32[64,32,128]{2,1,0:T(8,128)S(1)} %all_to_all.11.received), custom_call_target="tpu_custom_call" | custom-call | tf_op jit(solution)/shard_map/place/pallas_call | solution.py:137
Async XLA Ops:
  0.6 14.5 %copy-start = (bf16[1,2,64,2048]{3,2,1,0:T(8,128)(2,1)S(1)}, bf16[1,2,64,2048]{3,2,1,0:T(8,128)(2,1)}, u32[]{:S(2)}) copy-start(bf16[1,2,64,2048]{3,2,1,0:T(8,128)(2,1)} %param.10) | copy-start | bytes 1572868
  2.6 0.7 copy-start.8
  15.1 1.2 %copy-start.1 = (f32[1,2,64,2048]{3,2,1,0:T(8,128)S(1)}, f32[1,2,64,2048]{3,2,1,0:T(8,128)}, u32[]{:S(2)}) copy-start(f32[1,2,64,2048]{3,2,1,0:T(8,128)} %param.9) | copy-start | bytes 3145732
  16.4 1.2 %copy-start.2 = (f32[1,2,64,2048]{3,2,1,0:T(8,128)S(1)}, f32[1,2,64,2048]{3,2,1,0:T(8,128)}, u32[]{:S(2)}) copy-start(f32[1,2,64,2048]{3,2,1,0:T(8,128)} %param.11) | copy-start | bytes 3145732
  17.6 1.2 %copy-start.3 = (f32[1,2,64,2048]{3,2,1,0:T(8,128)S(1)}, f32[1,2,64,2048]{3,2,1,0:T(8,128)}, u32[]{:S(2)}) copy-start(f32[1,2,64,2048]{3,2,1,0:T(8,128)} %param.12) | copy-start | bytes 3145732
  21.2 40.6 %copy-start.4 = (f32[28,1,2048]{2,1,0:T(1,128)S(1)}, f32[28,1,2048]{2,1,0:T(1,128)}, u32[]{:S(2)}) copy-start(f32[28,1,2048]{2,1,0:T(1,128)} %param.13) | copy-start | bytes 688132
  21.2 40.6 %copy-start.5 = (f32[28,1,2048]{2,1,0:T(1,128)S(1)}, f32[28,1,2048]{2,1,0:T(1,128)}, u32[]{:S(2)}) copy-start(f32[28,1,2048]{2,1,0:T(1,128)} %param.14) | copy-start | bytes 688132
  61.9 0.7 copy-start.6
  61.9 0.7 copy-start.7

commit v2 on v1

v2 whole, which is shorter than its diff:
```python
import functools
import math

import jax
import jax.numpy as jnp
from jax import lax
from jax.experimental import pallas as pl
from jax.experimental.pallas import tpu as pltpu
from jax.sharding import PartitionSpec as P

LOW = 12
INNER_STEP = 500


BETA_FIRST = 0.9
BETA_SECOND = 0.95
LEARN_RATE = 0.0004
WEIGHT_DECAY = 0.1
ADAM_EPS = 1e-08
OUTER_RATE = 0.7
OUTER_MOMENTUM = 0.9
CLIP_SHARE = 0.2

LANES = 128
FIRST_FIX = 1.0 - BETA_FIRST**INNER_STEP
SECOND_FIX = 1.0 - BETA_SECOND**INNER_STEP


SPAN = 16


def load(sources, buffers, sems, step):
    level, rows = divmod(step * SPAN, sources[0].shape[1])
    copies = []
    for kind, (source, buffer) in enumerate(zip(sources, buffers)):
        at = (level, slice(rows, rows + SPAN))
        copies.append(pltpu.make_async_copy(source.at[at], buffer.at[at], sems.at[kind, step]))
    return copies


def norm_kernel(grads, partial, buffer, sems):
    levels, rows, width = grads.shape
    steps = levels * rows // SPAN
    copies = [load((grads,), (buffer,), sems, step)[0] for step in range(steps)]
    for copy in copies:
        copy.start()
    sums = [jnp.zeros((8, LANES), jnp.float32) for _ in range(4)]
    for step in range(steps):
        copies[step].wait()
        level, row = divmod(step * SPAN, rows)
        for chunk in range(width // LANES):
            part = buffer[level, row : row + SPAN, chunk * LANES : (chunk + 1) * LANES].astype(jnp.float32)
            for half in range(SPAN // 8):
                piece = part[half * 8 : half * 8 + 8]
                slot = (chunk * 2 + half) % 4
                sums[slot] = sums[slot] + piece * piece
    partial[...] = (sums[0] + sums[1]) + (sums[2] + sums[3])


def inner_kernel(
    clip_norm, near, far, decayed, grads, kept_mean, kept_square, new_mean, new_square, send, mean, square, sems
):
    levels, rows, width = decayed.shape
    chunks = width // LANES
    squares = jnp.sum(jnp.sum(near[...] + far[...], axis=0, keepdims=True), axis=1, keepdims=True)
    factor = jnp.minimum(1.0, clip_norm * lax.rsqrt(squares + 1e-06))
    factor = jnp.broadcast_to(factor, (SPAN, LANES))
    stores = []
    for step in range(levels * rows // SPAN):
        level, row = divmod(step * SPAN, rows)
        here = slice(row, row + SPAN)
        for chunk in range(chunks):
            at = (level, here, slice(chunk * LANES, (chunk + 1) * LANES))
            clipped = grads[at].astype(jnp.float32) * factor
            first = kept_mean[at] + (1.0 - BETA_FIRST) * clipped
            second = kept_square[at] + (1.0 - BETA_SECOND) * clipped * clipped
            mean[at] = first
            square[at] = second
            fixed = second * (1.0 / SECOND_FIX)
            root = fixed * lax.rsqrt(fixed) + ADAM_EPS
            update = first * (LEARN_RATE / FIRST_FIX) * pl.reciprocal(root, approx=True)
            send[here, level * chunks + chunk, :] = decayed[at] - update
        for kind, (source, target) in enumerate(((mean, new_mean), (square, new_square))):
            store = pltpu.make_async_copy(source.at[level, here], target.at[level, here], sems.at[kind, step])
            store.start()
            stores.append(store)
    for store in stores:
        store.wait()


def outer_kernel(
    low, high, tokens, received, anchor, momentum, new_anchor, new_moment, send, totals, *sums
):
    paths = received.shape[0]
    modules, chunks, _ = anchor.shape
    for each in sums:
        each[...] = jnp.zeros_like(each)
    for module in range(modules):
        totals[module] = 0
    lanes = len(sums) // 2

    def add(turn, carry):
        for lane in range(lanes):
            path = turn * lanes + lane
            count = tokens[path]
            weight = jnp.full((chunks, LANES), count, jnp.int32).astype(jnp.float32)
            one, two = low[path], high[path]
            sums[lane][one] += weight * received[path, :chunks, :]
            sums[lanes + lane][two] += weight * received[path, chunks:, :]
            totals[one] += count
            totals[two + LOW] += count
        return carry

    lax.fori_loop(0, paths // lanes, add, 0, unroll=2)
    for module in range(modules):
        total = jnp.full((chunks, LANES), totals[module], jnp.int32).astype(jnp.float32)
        old = anchor[module]
        if module < LOW:
            parts = [sums[lane][module] for lane in range(lanes)]
        else:
            parts = [sums[lanes + lane][module - LOW] for lane in range(lanes)]
        outer_grad = (total * old - sum(parts)) / jnp.maximum(total, 1.0)
        moment = OUTER_MOMENTUM * momentum[module] + outer_grad
        new_moment[module] = moment
        new_anchor[module] = old - OUTER_RATE * (outer_grad + OUTER_MOMENTUM * moment)

    def pick(path, carry):
        send[path, :chunks, :] = new_anchor[low[path]]
        send[path, chunks:, :] = new_anchor[high[path] + LOW]
        return carry

    lax.fori_loop(0, paths, pick, 0, unroll=8)


def place_kernel(received, new_params, placed, sems):
    levels, rows, width = new_params.shape
    chunks = width // LANES
    stores = []
    for step in range(levels * rows // SPAN):
        level, row = divmod(step * SPAN, rows)
        here = slice(row, row + SPAN)
        for chunk in range(chunks):
            lanes = slice(chunk * LANES, (chunk + 1) * LANES)
            placed[level, here, lanes] = received[here, level * chunks + chunk, :]
        store = pltpu.make_async_copy(placed.at[level, here], new_params.at[level, here], sems.at[step])
        store.start()
        stores.append(store)
    for store in stores:
        store.wait()


VMEM = pl.BlockSpec(memory_space=pltpu.VMEM)
SMEM = pl.BlockSpec(memory_space=pltpu.SMEM)
HBM = pl.BlockSpec(memory_space=pltpu.HBM)
ANY = pl.BlockSpec(memory_space=pl.ANY)


def shards(
    params, grads, adam_mean, adam_square, anchor, momentum, module_low, module_high, tok_counts
):
    _, levels, rows, width = params.shape
    modules = anchor.shape[0]
    paths = module_low.shape[0]
    chunks = width // LANES
    f32 = jnp.float32
    steps = levels * rows // SPAN
    grant = pltpu.CompilerParams(vmem_limit_bytes=16 * 1024 * 1024)
    local = jax.ShapeDtypeStruct((levels, rows, width), f32)
    wire = jax.ShapeDtypeStruct((rows, levels * chunks, LANES), f32)
    owned = jax.ShapeDtypeStruct((modules, chunks, LANES), f32)
    held = pltpu.VMEM((levels, rows, width), f32)
    held_grads = pltpu.VMEM((levels, rows, width), grads.dtype)
    partial = pl.pallas_call(
        norm_kernel,
        out_shape=jax.ShapeDtypeStruct((8, LANES), f32),
        in_specs=[HBM],
        out_specs=VMEM,
        scratch_shapes=[held_grads, pltpu.SemaphoreType.DMA((1, steps))],
        compiler_params=grant,
        name="norm",
    )(grads[0])
    shard_count = lax.axis_size("shard")
    near = partial + lax.ppermute(partial, "shard", [(i, i ^ 1) for i in range(shard_count)])
    far = lax.ppermute(near, "shard", [(i, i ^ 2) for i in range(shard_count)])
    clip_norm = CLIP_SHARE * math.sqrt(2 * rows * shard_count * width)
    decayed = params[0] * (1.0 - LEARN_RATE * WEIGHT_DECAY)
    kept_mean = BETA_FIRST * adam_mean[0]
    kept_square = BETA_SECOND * adam_square[0]
    new_mean, new_square, send = pl.pallas_call(
        functools.partial(inner_kernel, clip_norm),
        out_shape=(local, local, wire),
        in_specs=[VMEM] * 6,
        out_specs=(HBM, HBM, VMEM),
        scratch_shapes=[held, held, pltpu.SemaphoreType.DMA((2, steps))],
        compiler_params=grant,
        name="inner",
    )(near, far, decayed, grads[0], kept_mean, kept_square)
    received = lax.all_to_all(send, "path", 0, 0, tiled=True)
    new_anchor, new_moment, send_back = pl.pallas_call(
        outer_kernel,
        out_shape=(owned, owned, jax.ShapeDtypeStruct((paths, levels * chunks, LANES), f32)),
        in_specs=[SMEM] * 3 + [VMEM] * 3,
        out_specs=(VMEM,) * 3,
        scratch_shapes=[pltpu.SMEM((modules,), jnp.int32)]
        + [pltpu.VMEM((LOW, chunks, LANES), f32)] * 4 + [pltpu.VMEM((modules - LOW, chunks, LANES), f32)] * 4,
        compiler_params=grant,
        name="outer",
    )(
        module_low, module_high, tok_counts, received,
        anchor.reshape(modules, chunks, LANES), momentum.reshape(modules, chunks, LANES),
    )
    returned = lax.all_to_all(send_back, "path", 0, 0, tiled=True)
    new_params = pl.pallas_call(
        place_kernel,
        out_shape=local,
        in_specs=[VMEM],
        out_specs=HBM,
        scratch_shapes=[held, pltpu.SemaphoreType.DMA((steps,))],
        compiler_params=grant,
        name="place",
    )(returned)
    return (
        new_params[None], new_mean[None], new_square[None],
        new_anchor.reshape(anchor.shape), new_moment.reshape(anchor.shape),
    )


def solution(mesh):
    return jax.shard_map(
        shards,
        mesh=mesh,
        in_specs=(
            P("path", None, "shard", None),
            P("path", None, "shard", None),
            P("path", None, "shard", None),
            P("path", None, "shard", None),
            P(None, ("shard", "path"), None),
            P(None, ("shard", "path"), None),
            P(),
            P(),
            P(),
        ),
        out_specs=(
            P("path", None, "shard", None),
            P("path", None, "shard", None),
            P("path", None, "shard", None),
            P(None, ("shard", "path"), None),
            P(None, ("shard", "path"), None),
        ),
        check_vma=False,
    )
```

time: 99.7 us -> 91.8 us (0.921)
  blocking collectives: 82.7 us -> 75.5 us
  local copies, waits for them, and re-layouts: 5.58 us -> 1.73 us
  waiting for transfers between devices: 0 us -> 2.71 us
  starting transfers between devices: 0 us -> 2.47 us
  between operations: 2 us -> 0.74 us
    psum x1 -> x0, blocking collectives: 9.84 us -> none  [shards(): squares = lax.psum(jnp.sum(gradient * gradient), 'shard')]
    unnamed x18 -> x16, local copies, waits for them, and re-layouts: 5 us -> 1.73 us
    ppermute x0 -> x2, waiting for transfers between devices: none -> 2.71 us  [the longest x1 2.7 us: shards(): far = lax.ppermute(near, 'shard', [(i, i ^ 2) for i in range(shard_count)])]
    ppermute x0 -> x2, starting transfers between devices: none -> 2.47 us  [the longest x1 2.38 us: shards(): far = lax.ppermute(near, 'shard', [(i, i ^ 2) for i in range(shard_count)])]
    reduce_sum x1 -> x0, other arithmetic: 1.98 us -> none  [shards(): squares = lax.psum(jnp.sum(gradient * gradient), 'shard')]
    mul x0 -> x2, other arithmetic: none -> 1.91 us  [the longest x1 1.81 us: shards(): kept_square = BETA_SECOND * adam_square[0]]
    all_to_all x1, blocking collectives: 40.6 us -> 42.1 us  [shards(): received = lax.all_to_all(send, 'path', 0, 0, tiled=True)]
    all_to_all x1, blocking collectives: 32.2 us -> 33.4 us  [shards(): returned = lax.all_to_all(send_back, 'path', 0, 0, tiled=True)]
  transfers between devices with their start and end apart: 0 -> 2, of which waited for: 0 -> 1; matrix products, arithmetic and copies ran while one was open for 0% -> 2% of each run, Pallas kernels for 0% -> 0%
where the time goes in v2:
time: 91.8 us; the launch traced here: 91.6 us
  blocking collectives  75.5 us (82%)
  Pallas kernels  6.55 us (7%)
  waiting for transfers between devices  2.71 us (3%)
  starting transfers between devices  2.47 us (3%)
  other arithmetic  1.91 us (2%)
  local copies, waits for them, and re-layouts  1.73 us (2%)
    all_to_all x1, blocking collectives, shards(): received = lax.all_to_all(send, 'path', 0, 0, tiled=True)  42.1 us
    all_to_all x1, blocking collectives, shards(): returned = lax.all_to_all(send_back, 'path', 0, 0, tiled=True)  33.4 us
    ppermute x1, waiting for transfers between devices, shards(): far = lax.ppermute(near, 'shard', [(i, i ^ 2) for i in range(shard_count)])  2.7 us
    ppermute x1, starting transfers between devices, shards(): far = lax.ppermute(near, 'shard', [(i, i ^ 2) for i in range(shard_count)])  2.38 us
    pallas_call x1, Pallas kernels, shards(): pl.pallas_call(outer_kernel, out_shape=(owned, owned, jax.ShapeDtypeStruc...  2.23 us
    pallas_call x1, Pallas kernels, shards(): pl.pallas_call(functools.partial(inner_kernel, clip_norm), out_shape=(loc...  2.19 us
  transfers between devices with their start and end apart: 2, of which 1 were waited for; matrix products, arithmetic and copies ran while one was open for 2% of the time, Pallas kernels for 0%

profile of v2, /device:TPU:8, one launch (start us, length us, event | category | flops | bytes accessed | tf_op | source)
XLA Modules:
  0.0 91.6 jit_solution(15895646510186402518)
XLA Ops:
  0.6 0.0 copy-start
  0.6 1.0 %copy-done = bf16[1,2,64,2048]{3,2,1,0:T(8,128)(2,1)S(1)} copy-done((bf16[1,2,64,2048]{3,2,1,0:T(8,128)(2,1)S(1)}, bf16[1,2,64,2048]{3,2,1,0:T(8,128)(2,1)}, u32[]{:S(2)}) %copy-start) | copy-done | bytes 524312
  1.7 0.8 norm.1
  2.5 0.0 copy-start.7
  2.5 0.1 collective-permute-start
  2.6 1.8 %multiply_bitcast_fusion = (f32[2,64,2048]{2,1,0:T(8,128)S(1)}, f32[2,64,2048]{2,1,0:T(8,128)S(1)}) fusion(f32[1,2,64,2048]{3,2,1,0:T(8,128)} %param.12, f32[1,2,64,2048]{3,2,1,0:T(8,128)} %param.11), kind=kLoop, calls=%fused_computation | loop fusion | flops 524288 | bytes 4194304 | tf_op jit(solution)/shard_map/mul | solution.py:188
  4.4 0.0 collective-permute-done
  4.5 0.0 copy-start.1
  4.5 2.4 %collective-permute-start.1 = (f32[8,128]{1,0:T(8,128)S(1)}, f32[8,128]{1,0:T(8,128)S(1)}, u32[]{:S(2)}, u32[]{:S(2)}) collective-permute-start(f32[8,128]{1,0:T(8,128)S(1)} %add.3.near), channel_id=1, source_target_pairs={{0,2},{1,3},{2,0},{3,1},{4,6},{5,7},{6,4},{7,5},{8,10},{9,11},{10,... | collective-permute-start | bytes 12296 | tf_op jit(solution)/shard_map/ppermute | solution.py:184
  6.9 0.0 copy-done.7
  6.9 0.1 multiply_bitcast_fusion.2.decayed
  7.0 2.7 %collective-permute-done.1.far = f32[8,128]{1,0:T(8,128)S(1)} collective-permute-done((f32[8,128]{1,0:T(8,128)S(1)}, f32[8,128]{1,0:T(8,128)S(1)}, u32[]{:S(2)}, u32[]{:S(2)}) %collective-permute-start.1) | collective-permute-done | bytes 4128 | tf_op jit(solution)/shard_map/ppermute | solution.py:184
  9.7 0.0 copy-done.1
  9.7 2.2 %inner.1 = (f32[2,64,2048]{2,1,0:T(8,128)}, f32[2,64,2048]{2,1,0:T(8,128)}, f32[64,32,128]{2,1,0:T(8,128)S(1)}) custom-call(f32[8,128]{1,0:T(8,128)S(1)} %add.3.near, f32[8,128]{1,0:T(8,128)S(1)} %collective-permute-done.1.far, f32[2,64,2048]{2,1,0:T(8,128)S(1)} %multiply_bitcast_fusion.2.decayed, bf16[2,64,2048]{2,1,0:T(8,128)(2,1)S(1)} %bitcast.15, ...), custom_call_target="tpu_custom_call" | custom-call | tf_op jit(solution)/shard_map/inner/pallas_call | solution.py:189
  11.9 0.0 copy-start.2
  11.9 0.0 copy-start.3
  11.9 42.1 %all_to_all.10.received = f32[64,32,128]{2,1,0:T(8,128)S(1)} all-to-all(f32[64,32,128]{2,1,0:T(8,128)S(1)} %get-tuple-element.11), channel_id=1, replica_groups=mesh['path'=64,'shard'=4] {'path'}, dimensions={0} | all-to-all | bytes 2097152 | tf_op jit(solution)/shard_map/all_to_all | solution.py:198
  54.0 0.0 copy-start.4
  54.0 0.0 copy-start.5
  54.0 0.0 copy-start.6
  54.0 0.0 copy-done.2
  54.0 0.0 copy-done.3
  54.0 0.6 copy-done.4
  54.6 0.0 copy-done.5
  54.7 0.0 copy-done.6
  54.7 2.2 %outer.1 = (f32[28,16,128]{2,1,0:T(8,128)}, f32[28,16,128]{2,1,0:T(8,128)}, f32[64,32,128]{2,1,0:T(8,128)S(1)}) custom-call(s32[64]{0:T(128)S(1)} %copy-done.4, s32[64]{0:T(128)S(1)} %copy-done.5, s32[64]{0:T(128)S(1)} %copy-done.6, f32[64,32,128]{2,1,0:T(8,128)S(1)} %all_to_all.10.received, f32[28,16,128]{2,1,0:T(8,128)S(1)} %bitcast.16, ...), custom_call_target="tpu_custom_call" | custom-call | tf_op jit(solution)/shard_map/outer/pallas_call | solution.py:199
  56.9 33.4 %all_to_all.11.received = f32[64,32,128]{2,1,0:T(8,128)S(1)} all-to-all(f32[64,32,128]{2,1,0:T(8,128)S(1)} %get-tuple-element.12), channel_id=1, replica_groups=mesh['path'=64,'shard'=4] {'path'}, dimensions={0} | all-to-all | bytes 2097152 | tf_op jit(solution)/shard_map/all_to_all | solution.py:212
  90.3 1.3 %place.1 = f32[2,64,2048]{2,1,0:T(8,128)} custom-call(f32[64,32,128]{2,1,0:T(8,128)S(1)} %all_to_all.11.received), custom_call_target="tpu_custom_call" | custom-call | tf_op jit(solution)/shard_map/place/pallas_call | solution.py:213
  (1 shorter events, 0.0 us)
Async XLA Ops:
  0.6 1.0 %copy-start = (bf16[1,2,64,2048]{3,2,1,0:T(8,128)(2,1)S(1)}, bf16[1,2,64,2048]{3,2,1,0:T(8,128)(2,1)}, u32[]{:S(2)}) copy-start(bf16[1,2,64,2048]{3,2,1,0:T(8,128)(2,1)} %param.10) | copy-start | bytes 1572868
  2.5 4.3 %copy-start.7 = (f32[1,2,64,2048]{3,2,1,0:T(8,128)S(1)}, f32[1,2,64,2048]{3,2,1,0:T(8,128)}, u32[]{:S(2)}) copy-start(f32[1,2,64,2048]{3,2,1,0:T(8,128)} %param.9) | copy-start | bytes 3145732
  2.5 1.9 %collective-permute-start = (f32[8,128]{1,0:T(8,128)S(1)}, f32[8,128]{1,0:T(8,128)S(1)}, u32[]{:S(2)}, u32[]{:S(2)}) collective-permute-start(f32[8,128]{1,0:T(8,128)S(1)} %norm.1), channel_id=1, source_target_pairs={{0,1},{1,0},{2,3},{3,2},{4,5},{5,4},{6,7},{7,6},{8,9},{9,8},{10,11... | collective-permute-start | bytes 12296 | tf_op jit(solution)/shard_map/ppermute | solution.py:183
  4.5 5.2 %copy-start.1 = (bf16[1,2,64,2048]{3,2,1,0:T(8,128)(2,1)S(1)}, bf16[1,2,64,2048]{3,2,1,0:T(8,128)(2,1)}, u32[]{:S(2)}) copy-start(bf16[1,2,64,2048]{3,2,1,0:T(8,128)(2,1)} %param.10) | copy-start | bytes 1572868
  4.5 5.2 %collective-permute-start.1 = (f32[8,128]{1,0:T(8,128)S(1)}, f32[8,128]{1,0:T(8,128)S(1)}, u32[]{:S(2)}, u32[]{:S(2)}) collective-permute-start(f32[8,128]{1,0:T(8,128)S(1)} %add.3.near), channel_id=1, source_target_pairs={{0,2},{1,3},{2,0},{3,1},{4,6},{5,7},{6,4},{7,5},{8,10},{9,11},{10,... | collective-permute-start | bytes 12296 | tf_op jit(solution)/shard_map/ppermute | solution.py:184
  11.9 42.1 %copy-start.2 = (f32[28,1,2048]{2,1,0:T(1,128)S(1)}, f32[28,1,2048]{2,1,0:T(1,128)}, u32[]{:S(2)}) copy-start(f32[28,1,2048]{2,1,0:T(1,128)} %param.13) | copy-start | bytes 688132
  11.9 42.1 %copy-start.3 = (f32[28,1,2048]{2,1,0:T(1,128)S(1)}, f32[28,1,2048]{2,1,0:T(1,128)}, u32[]{:S(2)}) copy-start(f32[28,1,2048]{2,1,0:T(1,128)} %param.14) | copy-start | bytes 688132
  54.0 0.7 copy-start.4
  54.0 0.7 copy-start.5
  54.0 0.7 copy-start.6

commit v3 on v0

v3 whole, which is shorter than its diff:
```python
import functools
import math

import jax
import jax.numpy as jnp
from jax import lax
from jax.experimental import pallas as pl
from jax.experimental.pallas import tpu as pltpu
from jax.sharding import PartitionSpec as P

LOW = 12
INNER_STEP = 500


BETA_FIRST = 0.9
BETA_SECOND = 0.95
LEARN_RATE = 0.0004
WEIGHT_DECAY = 0.1
ADAM_EPS = 1e-08
OUTER_RATE = 0.7
OUTER_MOMENTUM = 0.9
CLIP_SHARE = 0.2

LANES = 128
SPAN = 16
LANES_OF_SUMS = 2
FIRST_FIX = 1.0 - BETA_FIRST**INNER_STEP
SECOND_FIX = 1.0 - BETA_SECOND**INNER_STEP

VMEM = pl.BlockSpec(memory_space=pltpu.VMEM)
SMEM = pl.BlockSpec(memory_space=pltpu.SMEM)
HBM = pl.BlockSpec(memory_space=pltpu.HBM)


def tiles(shape):
    levels, rows, width = shape
    for step in range(levels * rows // SPAN):
        level, row = divmod(step * SPAN, rows)
        here = slice(row, row + SPAN)
        yield step, level, here, places(level, here, width)


def places(level, here, width):
    return [(chunk, (level, here, slice(chunk * LANES, (chunk + 1) * LANES))) for chunk in range(width // LANES)]


def norm_kernel(grads, partial, buffer, sems):
    copies = []
    for step, level, here, _ in tiles(grads.shape):
        copies.append(pltpu.make_async_copy(grads.at[level, here], buffer.at[level, here], sems.at[step]))
        copies[-1].start()
    sums = [jnp.zeros((8, LANES), jnp.float32) for _ in range(4)]
    for step, _, _, spots in tiles(grads.shape):
        copies[step].wait()
        for chunk, at in spots:
            part = buffer[at].astype(jnp.float32)
            for half in range(SPAN // 8):
                piece = part[half * 8 : half * 8 + 8]
                slot = (chunk * 2 + half) % 4
                sums[slot] = sums[slot] + piece * piece
    partial[...] = (sums[0] + sums[1]) + (sums[2] + sums[3])


def prepare_kernel(ids, anchor, momentum, scaled, inverse, kept_moment, totals):
    modules, chunks, _ = anchor.shape
    paths = ids.shape[0] // 3
    for module in range(modules):
        totals[module] = 0

    def add(path, carry):
        count = ids[2 * paths + path]
        totals[ids[path]] += count
        totals[ids[paths + path] + LOW] += count
        return carry

    lax.fori_loop(0, paths, add, 0, unroll=8)
    for module in range(modules):
        total = jnp.full((chunks, LANES), totals[module], jnp.int32).astype(jnp.float32)
        scaled[module] = total * anchor[module]
        inverse[module] = 1.0 / jnp.maximum(total, 1.0)
        kept_moment[module] = OUTER_MOMENTUM * momentum[module]


def clip_factor(clip_norm, near, far):
    squares = jnp.sum(jnp.sum(near[...] + far[...], axis=0, keepdims=True), axis=1, keepdims=True)
    factor = jnp.minimum(1.0, clip_norm * lax.rsqrt(squares + 1e-06))
    return jnp.broadcast_to(factor, (SPAN, LANES))


def moments(at, factor, grads, kept_mean, kept_square):
    clipped = grads[at].astype(jnp.float32) * factor
    first = kept_mean[at] + (1.0 - BETA_FIRST) * clipped
    second = kept_square[at] + (1.0 - BETA_SECOND) * clipped * clipped
    return first, second


def stepped(first, second, decayed):
    fixed = second * (1.0 / SECOND_FIX)
    root = fixed * lax.rsqrt(fixed) + ADAM_EPS
    return decayed - first * (LEARN_RATE / FIRST_FIX) * pl.reciprocal(root, approx=True)


def write_moments(step, level, here, mean, square, new_mean, new_square, sems):
    stores = []
    for kind, (source, target) in enumerate(((mean, new_mean), (square, new_square))):
        store = pltpu.make_async_copy(source.at[level, here], target.at[level, here], sems.at[kind, step])
        store.start()
        stores.append(store)
    return stores


def lead_kernel(clip_norm, near, far, decayed, grads, kept_mean, kept_square, send):
    factor = clip_factor(clip_norm, near, far)
    for _, level, here, spots in tiles(decayed.shape):
        for chunk, at in spots:
            first, second = moments(at, factor, grads, kept_mean, kept_square)
            send[here, level * len(spots) + chunk, :] = stepped(first, second, decayed[at])


def moment_kernel(clip_norm, near, far, grads, kept_mean, kept_square, new_mean, new_square, mean, square, sems):
    factor = clip_factor(clip_norm, near, far)
    stores = []
    for step, level, here, spots in tiles(grads.shape):
        for _, at in spots:
            mean[at], square[at] = moments(at, factor, grads, kept_mean, kept_square)
        stores += write_moments(step, level, here, mean, square, new_mean, new_square, sems)
    for store in stores:
        store.wait()


def follow_kernel(
    clip_norm, near, far, decayed, grads, kept_mean, kept_square,
    new_mean, new_square, given, kept, mean, square, sems,
):
    factor = clip_factor(clip_norm, near, far)
    levels, rows, width = decayed.shape
    half = rows // 2
    mine = lax.axis_index("path") // half
    stores = []
    step = 0
    for send, side in ((given, 1 - mine), (kept, mine)):
        for row in range(0, half, SPAN):
            here = pl.ds(pl.multiple_of(side * half + row, SPAN), SPAN)
            for level in range(levels):
                spots = places(level, here, width)
                for chunk, at in spots:
                    first, second = moments(at, factor, grads, kept_mean, kept_square)
                    mean[at] = first
                    square[at] = second
                    send[row : row + SPAN, level * len(spots) + chunk, :] = stepped(first, second, decayed[at])
                stores += write_moments(step, level, here, mean, square, new_mean, new_square, sems)
                step += 1
    for store in stores:
        store.wait()


def outer_kernel(
    ids, received, anchor, scaled, inverse, kept_moment, new_anchor, new_moment, send,
    anchor_held, moment_held, sems, *sums,
):
    paths = ids.shape[0] // 3
    rows = received.shape[0]
    modules, chunks, _ = anchor.shape
    first_side = lax.axis_index("path") // rows if rows < paths else 0
    for each in sums:
        each[...] = jnp.zeros_like(each)
    for path in range(paths):
        lane = path % LANES_OF_SUMS
        weight = jnp.full((chunks, LANES), ids[2 * paths + path], jnp.int32).astype(jnp.float32)
        side, row = divmod(path, rows)
        slot = side ^ first_side
        sums[lane][ids[path]] += weight * received[row, slot, :chunks, :]
        sums[LANES_OF_SUMS + lane][ids[paths + path]] += weight * received[row, slot, chunks:, :]
    for module in range(modules):
        start, place = (0, module) if module < LOW else (LANES_OF_SUMS, module - LOW)
        summed = sum(sums[start + lane][place] for lane in range(LANES_OF_SUMS))
        outer_grad = (scaled[module] - summed) * inverse[module]
        moment = kept_moment[module] + outer_grad
        moment_held[module] = moment
        anchor_held[module] = anchor[module] - OUTER_RATE * (outer_grad + OUTER_MOMENTUM * moment)
    stores = [
        pltpu.make_async_copy(anchor_held, new_anchor, sems.at[0]),
        pltpu.make_async_copy(moment_held, new_moment, sems.at[1]),
    ]
    for store in stores:
        store.start()
    for path in range(paths):
        send[path, :chunks, :] = anchor_held[ids[path]]
        send[path, chunks:, :] = anchor_held[ids[paths + path] + LOW]
    for store in stores:
        store.wait()


def place_kernel(received, new_params, placed, sems):
    stores = []
    for step, level, here, spots in tiles(new_params.shape):
        for chunk, at in spots:
            placed[at] = received[here, level * len(spots) + chunk, :]
        store = pltpu.make_async_copy(placed.at[level, here], new_params.at[level, here], sems.at[step])
        store.start()
        stores.append(store)
    for store in stores:
        store.wait()


def shards(
    params, grads, adam_mean, adam_square, anchor, momentum, module_low, module_high, tok_counts
):
    _, levels, rows, width = params.shape
    modules = anchor.shape[0]
    paths = module_low.shape[0]
    chunks = width // LANES
    steps = levels * rows // SPAN
    f32 = jnp.float32
    grant = pltpu.CompilerParams(vmem_limit_bytes=16 * 1024 * 1024)
    local = jax.ShapeDtypeStruct((levels, rows, width), f32)
    wire = jax.ShapeDtypeStruct((rows, levels * chunks, LANES), f32)
    half_wire = jax.ShapeDtypeStruct((rows // 2, levels * chunks, LANES), f32)
    owned = jax.ShapeDtypeStruct((modules, chunks, LANES), f32)
    held = pltpu.VMEM((levels, rows, width), f32)
    pair_sems = pltpu.SemaphoreType.DMA((2, steps))
    ids = jnp.concatenate([module_low, module_high, tok_counts])

    partial = pl.pallas_call(
        norm_kernel,
        out_shape=jax.ShapeDtypeStruct((8, LANES), f32),
        in_specs=[HBM],
        out_specs=VMEM,
        scratch_shapes=[pltpu.VMEM((levels, rows, width), grads.dtype), pltpu.SemaphoreType.DMA((steps,))],
        compiler_params=grant,
        name="norm",
    )(grads[0])
    shard_count = lax.axis_size("shard")
    near = partial + lax.ppermute(partial, "shard", [(i, i ^ 1) for i in range(shard_count)])
    far = lax.ppermute(near, "shard", [(i, i ^ 2) for i in range(shard_count)])
    clip_norm = CLIP_SHARE * math.sqrt(2 * rows * shard_count * width)

    kept_mean = BETA_FIRST * adam_mean[0]
    kept_square = BETA_SECOND * adam_square[0]
    decayed = params[0] * (1.0 - LEARN_RATE * WEIGHT_DECAY)
    gradient = grads[0]
    staged = (decayed, kept_mean, kept_square)
    old_anchor = anchor.reshape(modules, chunks, LANES)
    prepared = pl.pallas_call(
        prepare_kernel,
        out_shape=(owned,) * 3,
        in_specs=[SMEM] + [VMEM] * 2,
        out_specs=(VMEM,) * 3,
        scratch_shapes=[pltpu.SMEM((modules,), jnp.int32)],
        compiler_params=grant,
        name="prepare",
    )(ids, old_anchor, momentum.reshape(modules, chunks, LANES))
    prepared = lax.optimization_barrier(prepared)

    def update(received):
        new_anchor, new_moment, send_back = pl.pallas_call(
            outer_kernel,
            out_shape=(owned, owned, jax.ShapeDtypeStruct((paths, levels * chunks, LANES), f32)),
            in_specs=[SMEM] + [VMEM] * 5,
            out_specs=(HBM, HBM, VMEM),
            scratch_shapes=[pltpu.VMEM((modules, chunks, LANES), f32)] * 2 + [pltpu.SemaphoreType.DMA((2,))]
            + [pltpu.VMEM((LOW, chunks, LANES), f32)] * LANES_OF_SUMS
            + [pltpu.VMEM((modules - LOW, chunks, LANES), f32)] * LANES_OF_SUMS,
            compiler_params=grant,
            name="outer",
        )(ids, received, old_anchor, *prepared)
        return lax.all_to_all(send_back, "path", 0, 0, tiled=True), new_anchor, new_moment

    def lead():
        send = pl.pallas_call(
            functools.partial(lead_kernel, clip_norm),
            out_shape=wire,
            in_specs=[VMEM] * 6,
            out_specs=VMEM,
            compiler_params=grant,
            name="lead",
        )(near, far, staged[0], gradient, *staged[1:])
        received = lax.all_to_all(send, "path", 0, 0, tiled=True)
        returned, new_anchor, new_moment = update(received.reshape(rows, 1, levels * chunks, LANES))
        first, second, _ = lax.optimization_barrier((*staged[1:], returned))
        new_mean, new_square = pl.pallas_call(
            functools.partial(moment_kernel, clip_norm),
            out_shape=(local, local),
            in_specs=[VMEM] * 5,
            out_specs=(HBM, HBM),
            scratch_shapes=[held, held, pair_sems],
            compiler_params=grant,
            name="moment",
        )(near, far, gradient, first, second)
        return returned, new_mean, new_square, new_anchor, new_moment

    def follow():
        new_mean, new_square, given, kept = pl.pallas_call(
            functools.partial(follow_kernel, clip_norm),
            out_shape=(local, local, half_wire, half_wire),
            in_specs=[VMEM] * 6,
            out_specs=(HBM, HBM, VMEM, VMEM),
            scratch_shapes=[held, held, pair_sems],
            compiler_params=grant,
            name="follow",
        )(near, far, staged[0], gradient, *staged[1:])
        half = paths // 2
        taken = lax.ppermute(given, "path", [(p, (p + half) % paths) for p in range(paths)])
        pair = jnp.stack([kept, taken], axis=1)
        groups = [list(range(half)), list(range(half, paths))]
        received = lax.all_to_all(pair, "path", 0, 0, axis_index_groups=groups, tiled=True)
        returned, new_anchor, new_moment = update(received)
        return returned, new_mean, new_square, new_anchor, new_moment

    leads = lax.rem(lax.axis_index("shard"), 2) == 1
    returned, new_mean, new_square, new_anchor, new_moment = lax.cond(leads, lead, follow)
    new_params = pl.pallas_call(
        place_kernel,
        out_shape=local,
        in_specs=[VMEM],
        out_specs=HBM,
        scratch_shapes=[held, pltpu.SemaphoreType.DMA((steps,))],
        compiler_params=grant,
        name="place",
    )(returned)
    return (
        new_params[None], new_mean[None], new_square[None],
        new_anchor.reshape(anchor.shape), new_moment.reshape(anchor.shape),
    )


def solution(mesh):
    return jax.shard_map(
        shards,
        mesh=mesh,
        in_specs=(
            P("path", None, "shard", None),
            P("path", None, "shard", None),
            P("path", None, "shard", None),
            P("path", None, "shard", None),
            P(None, ("shard", "path"), None),
            P(None, ("shard", "path"), None),
            P(),
            P(),
            P(),
        ),
        out_specs=(
            P("path", None, "shard", None),
            P("path", None, "shard", None),
            P("path", None, "shard", None),
            P(None, ("shard", "path"), None),
            P(None, ("shard", "path"), None),
        ),
        check_vma=False,
    )
```

time: 760 us -> 81.8 us (0.11)
  waiting for transfers between devices: 679 us -> 8.24 us
  blocking collectives: 9.8 us -> 56.5 us
  local copies, waits for them, and re-layouts: 28.4 us -> 0.04 us
  matrix products: 16 us -> 0 us
  between operations: 14.8 us -> 0.74 us
  other arithmetic: 11.3 us -> 2.17 us
  Pallas kernels: 0 us -> 8.93 us
    reduce_scatter x1 -> x0, waiting for transfers between devices: 355 us -> none  [shards(): lax.psum_scatter(partial_terms, 'path', scatter_dimension=1, tiled=True)]
    all_gather x1 -> x0, waiting for transfers between devices: 324 us -> none  [shards(): lax.all_gather(new_anchor, 'path', axis=1, tiled=True)]
    all_to_all x0 -> x2, blocking collectives: none -> 56.5 us  [the longest x1 30.6 us: follow(): lax.all_to_all(pair, 'path', 0, 0, axis_index_groups=groups, tiled=True)]
    all_gather x1 -> x0, local copies, waits for them, and re-layouts: 19.5 us -> none  [shards(): lax.all_gather(new_anchor, 'path', axis=1, tiled=True)]
    dot_general x1 -> x0, matrix products: 16 us -> none  [shards(): jnp.einsum('ml,lrd->mrd', own_weights, stepped[0], precision=lax.Precisio...]
    psum x1 -> x0, blocking collectives: 9.8 us -> none  [shards(): squares = lax.psum(local_squares, 'shard')]
    pallas_call x0 -> x5, Pallas kernels: none -> 8.93 us  [the longest x1 3.22 us: follow(): pl.pallas_call(functools.partial(follow_kernel, clip_norm), out_shape=(lo...]
    ppermute x0 -> x3, waiting for transfers between devices: none -> 8.24 us  [the longest x1 7.16 us: follow(): lax.ppermute(given, 'path', [(p, (p + half) % paths) for p in range(paths)])]
  transfers between devices with their start and end apart: 2 -> 3, of which waited for: 2 -> 2; matrix products, arithmetic and copies ran while one was open for 0% -> 3% of each run, Pallas kernels for 0% -> 2%
where the time goes in v3:
time: 81.8 us; the launch traced here: 81.4 us
  blocking collectives  56.5 us (69%)
  Pallas kernels  8.93 us (11%)
  waiting for transfers between devices  8.24 us (10%)
  starting transfers between devices  4.75 us (6%)
  other arithmetic  2.17 us (3%)
    all_to_all x1, blocking collectives, follow(): lax.all_to_all(pair, 'path', 0, 0, axis_index_groups=groups, tiled=True)  30.6 us
    all_to_all x1, blocking collectives, update(): lax.all_to_all(send_back, 'path', 0, 0, tiled=True)  26 us
    ppermute x1, waiting for transfers between devices, follow(): lax.ppermute(given, 'path', [(p, (p + half) % paths) for p in range(paths)])  7.16 us
    pallas_call x1, Pallas kernels, follow(): pl.pallas_call(functools.partial(follow_kernel, clip_norm), out_shape=(lo...  3.22 us
    ppermute x1, starting transfers between devices, shards(): far = lax.ppermute(near, 'shard', [(i, i ^ 2) for i in range(shard_count)])  2.38 us
    ppermute x1, starting transfers between devices, follow(): lax.ppermute(given, 'path', [(p, (p + half) % paths) for p in range(paths)])  2.27 us
    mul x1, other arithmetic, shards(): kept_square = BETA_SECOND * adam_square[0]  1.9 us
    pallas_call x1, Pallas kernels, shards(): pl.pallas_call(prepare_kernel, out_shape=(owned,) * 3, in_specs=[SMEM] +...  1.65 us
  transfers between devices with their start and end apart: 3, of which 2 were waited for; matrix products, arithmetic and copies ran while one was open for 3% of the time, Pallas kernels for 2%

profile of v3, /device:TPU:8, one launch (start us, length us, event | category | flops | bytes accessed | tf_op | source)
XLA Modules:
  0.0 81.4 jit_solution(104858856970718798)
XLA Ops:
  0.6 1.1 %norm.1 = f32[8,128]{1,0:T(8,128)S(1)} custom-call(bf16[2,64,2048]{2,1,0:T(8,128)(2,1)} %bitcast.20), custom_call_target="tpu_custom_call" | custom-call | tf_op jit(solution)/shard_map/norm/pallas_call | solution.py:224
  1.8 0.0 copy-start.3
  1.8 0.1 collective-permute-start.1
  1.9 1.9 %multiply_bitcast_fusion = (f32[2,64,2048]{2,1,0:T(8,128)S(1)}, f32[2,64,2048]{2,1,0:T(8,128)S(1)}) fusion(f32[1,2,64,2048]{3,2,1,0:T(8,128)} %param.14, f32[1,2,64,2048]{3,2,1,0:T(8,128)} %param.13), kind=kLoop, calls=%fused_computation.1 | loop fusion | flops 524288 | bytes 4194304 | tf_op jit(solution)/shard_map/mul | solution.py:239
  3.8 0.0 copy-done.3
  3.8 0.0 copy-start
  3.8 0.1 multiply_bitcast_fusion.2
  3.9 0.0 copy-start.4
  4.0 0.0 copy-start.5
  4.0 0.0 copy-start.6
  4.0 0.0 collective-permute-done.1
  4.0 2.4 %collective-permute-start.2 = (f32[8,128]{1,0:T(8,128)S(1)}, f32[8,128]{1,0:T(8,128)S(1)}, u32[]{:S(2)}, u32[]{:S(2)}) collective-permute-start(f32[8,128]{1,0:T(8,128)S(1)} %add.3), channel_id=1, source_target_pairs={{0,2},{1,3},{2,0},{3,1},{4,6},{5,7},{6,4},{7,5},{8,10},{9,11},{10,... | collective-permute-start | bytes 12296 | tf_op jit(solution)/shard_map/ppermute | solution.py:235
  6.4 0.0 copy-done.4
  6.4 0.0 copy-done.5
  6.4 0.0 copy-done.6
  6.4 0.1 pad_add_fusion.ids
  6.5 0.0 copy-done
  6.5 0.0 copy-start.2
  6.5 1.6 %prepare.1 = (f32[28,16,128]{2,1,0:T(8,128)S(1)}, f32[28,16,128]{2,1,0:T(8,128)S(1)}, f32[28,16,128]{2,1,0:T(8,128)S(1)}) custom-call(s32[192]{0:T(256)S(1)} %pad_add_fusion.ids, f32[28,16,128]{2,1,0:T(8,128)} %bitcast.23, f32[28,16,128]{2,1,0:T(8,128)S(1)} %bitcast.19), custom_call_target="tpu_custom_call" | custom-call | tf_op jit(solution)/shard_map/prepare/pallas_call | solution.py:244
  8.1 1.1 %collective-permute-done.2 = f32[8,128]{1,0:T(8,128)S(1)} collective-permute-done((f32[8,128]{1,0:T(8,128)S(1)}, f32[8,128]{1,0:T(8,128)S(1)}, u32[]{:S(2)}, u32[]{:S(2)}) %collective-permute-start.2) | collective-permute-done | bytes 4128 | tf_op jit(solution)/shard_map/ppermute | solution.py:235
  9.2 0.0 copy-done.2
  9.2 70.9 %conditional.1 = (f32[64,32,128]{2,1,0:T(8,128)S(1)}, f32[2,64,2048]{2,1,0:T(8,128)}, f32[2,64,2048]{2,1,0:T(8,128)}, f32[28,16,128]{2,1,0:T(8,128)}, f32[28,16,128]{2,1,0:T(8,128)}) conditional(s32[]{:T(128)} %convert_element_type.3, (f32[8,128]{1,0:T(8,128)S(1)}, f32[8,128]{1,0:T(8,128)S(1)}, f32[2,64,2048]{2,1,0:T(8,128)S(1)}, ...), branch_computations={%region_0.0_spmd, %region_1.0_spmd} | conditional | flops 262144 | bytes 8388688 | solution.py:311
  9.2 3.2 %follow.1 = (f32[2,64,2048]{2,1,0:T(8,128)}, f32[2,64,2048]{2,1,0:T(8,128)}, f32[32,32,128]{2,1,0:T(8,128)S(1)}, f32[32,32,128]{2,1,0:T(8,128)S(1)}) custom-call(f32[8,128]{1,0:T(8,128)S(1)} %get-tuple-element.45.near, f32[8,128]{1,0:T(8,128)S(1)} %get-tuple-element.46.far, f32[2,64,2048]{2,1,0:T(8,128)S(1)} %get-tuple-element.47.decayed, ...), custom_call_target="tpu_custom_call" | custom-call | tf_op jit(solution)/shard_map/cond/branch_0_fun/follow/pallas_call | solution.py:293
  12.4 2.3 %collective-permute-start = (f32[32,32,128]{2,1,0:T(8,128)S(1)}, f32[32,32,128]{2,1,0:T(8,128)S(1)}, u32[]{:S(2)}, u32[]{:S(2)}) collective-permute-start(f32[32,32,128]{2,1,0:T(8,128)S(1)} %get-tuple-element.52), channel_id=1, source_target_pairs={{0,128},{4,132},{8,136},{12,140},{16,144},{20,148},{24,152},{28,15... | collective-permute-start | bytes 1572872 | tf_op jit(solution)/shard_map/cond/branch_0_fun/ppermute | solution.py:303
  14.7 7.2 %collective-permute-done = f32[32,32,128]{2,1,0:T(8,128)S(1)} collective-permute-done((f32[32,32,128]{2,1,0:T(8,128)S(1)}, f32[32,32,128]{2,1,0:T(8,128)S(1)}, u32[]{:S(2)}, u32[]{:S(2)}) %collective-permute-start) | collective-permute-done | bytes 524320 | tf_op jit(solution)/shard_map/cond/branch_0_fun/ppermute | solution.py:303
  21.9 0.1 pad_maximum_fusion
  22.0 30.6 %all_to_all.16.received = f32[32,2,32,128]{3,2,1,0:T(8,128)S(1)} all-to-all(f32[32,2,32,128]{3,2,1,0:T(8,128)S(1)} %pad_maximum_fusion), channel_id=1, replica_groups={{0,4,8,12,16,20,24,28,32,36,40,44,48,52,56,60,64,68,72,76,80,84,88,92,9..., dimensions={0} | all-to-all | bytes 2097152 | tf_op jit(solution)/shard_map/cond/branch_0_fun/all_to_all | solution.py:306
  52.6 1.6 %outer.2 = (f32[28,16,128]{2,1,0:T(8,128)}, f32[28,16,128]{2,1,0:T(8,128)}, f32[64,32,128]{2,1,0:T(8,128)S(1)}) custom-call(s32[192]{0:T(256)S(1)} %get-tuple-element.44.ids, f32[32,2,32,128]{3,2,1,0:T(8,128)S(1)} %all_to_all.16.received, f32[28,16,128]{2,1,0:T(8,128)S(1)} %get-tuple-element.53.anchor, f32[28,16,128]{2,1,0:T(8,128)S(1)} %get-tuple-element.54.scaled, ...), custom_call_target="tpu_custom_call" | custom-call | tf_op jit(solution)/shard_map/cond/branch_0_fun/outer/pallas_call | solution.py:256
  54.2 26.0 %all_to_all.17 = f32[64,32,128]{2,1,0:T(8,128)S(1)} all-to-all(f32[64,32,128]{2,1,0:T(8,128)S(1)} %get-tuple-element.57), channel_id=1, replica_groups=mesh['path'=64,'shard'=4] {'path'}, dimensions={0} | all-to-all | bytes 2097152 | tf_op jit(solution)/shard_map/cond/branch_0_fun/all_to_all | solution.py:267
  80.1 1.3 %place.1 = f32[2,64,2048]{2,1,0:T(8,128)} custom-call(f32[64,32,128]{2,1,0:T(8,128)S(1)} %get-tuple-element.96.received), custom_call_target="tpu_custom_call" | custom-call | tf_op jit(solution)/shard_map/place/pallas_call | solution.py:312
  (1 shorter events, 0.0 us)
Async XLA Ops:
  1.8 2.0 %copy-start.3 = (f32[1,2,64,2048]{3,2,1,0:T(8,128)S(1)}, f32[1,2,64,2048]{3,2,1,0:T(8,128)}, u32[]{:S(2)}) copy-start(f32[1,2,64,2048]{3,2,1,0:T(8,128)} %param.11) | copy-start | bytes 3145732
  1.8 2.2 %collective-permute-start.1 = (f32[8,128]{1,0:T(8,128)S(1)}, f32[8,128]{1,0:T(8,128)S(1)}, u32[]{:S(2)}, u32[]{:S(2)}) collective-permute-start(f32[8,128]{1,0:T(8,128)S(1)} %norm.1), channel_id=1, source_target_pairs={{0,1},{1,0},{2,3},{3,2},{4,5},{5,4},{6,7},{7,6},{8,9},{9,8},{10,11... | collective-permute-start | bytes 12296 | tf_op jit(solution)/shard_map/ppermute | solution.py:234
  3.8 2.6 %copy-start = (f32[28,1,2048]{2,1,0:T(1,128)S(1)}, f32[28,1,2048]{2,1,0:T(1,128)}, u32[]{:S(2)}) copy-start(f32[28,1,2048]{2,1,0:T(1,128)} %param.16) | copy-start | bytes 688132
  3.9 2.4 %copy-start.4 = (s32[64]{0:T(128)S(1)}, s32[64]{0:T(128)}, u32[]{:S(2)}) copy-start(s32[64]{0:T(128)} %param.19) | copy-start | bytes 772
  4.0 2.4 %copy-start.5 = (s32[64]{0:T(128)S(1)}, s32[64]{0:T(128)}, u32[]{:S(2)}) copy-start(s32[64]{0:T(128)} %param.18) | copy-start | bytes 772
  4.0 2.4 %copy-start.6 = (s32[64]{0:T(128)S(1)}, s32[64]{0:T(128)}, u32[]{:S(2)}) copy-start(s32[64]{0:T(128)} %param.17) | copy-start | bytes 772
  4.0 5.2 %collective-permute-start.2 = (f32[8,128]{1,0:T(8,128)S(1)}, f32[8,128]{1,0:T(8,128)S(1)}, u32[]{:S(2)}, u32[]{:S(2)}) collective-permute-start(f32[8,128]{1,0:T(8,128)S(1)} %add.3), channel_id=1, source_target_pairs={{0,2},{1,3},{2,0},{3,1},{4,6},{5,7},{6,4},{7,5},{8,10},{9,11},{10,... | collective-permute-start | bytes 12296 | tf_op jit(solution)/shard_map/ppermute | solution.py:235
  6.5 2.7 %copy-start.2 = (f32[28,1,2048]{2,1,0:T(1,128)S(1)}, f32[28,1,2048]{2,1,0:T(1,128)}, u32[]{:S(2)}) copy-start(f32[28,1,2048]{2,1,0:T(1,128)} %param.15) | copy-start | bytes 688132
  12.4 9.4 %collective-permute-start = (f32[32,32,128]{2,1,0:T(8,128)S(1)}, f32[32,32,128]{2,1,0:T(8,128)S(1)}, u32[]{:S(2)}, u32[]{:S(2)}) collective-permute-start(f32[32,32,128]{2,1,0:T(8,128)S(1)} %get-tuple-element.52), channel_id=1, source_target_pairs={{0,128},{4,132},{8,136},{12,140},{16,144},{20,148},{24,152},{28,15... | collective-permute-start | bytes 1572872 | tf_op jit(solution)/shard_map/cond/branch_0_fun/ppermute | solution.py:303

commit v4 on v3

--- a/solution.py
+++ b/solution.py
@@ -128,16 +128,11 @@
         store.wait()
 
 
-def follow_kernel(
-    clip_norm, near, far, decayed, grads, kept_mean, kept_square,
-    new_mean, new_square, given, kept, mean, square, sems,
-):
+def follow_kernel(clip_norm, near, far, decayed, grads, kept_mean, kept_square, given, kept):
     factor = clip_factor(clip_norm, near, far)
     levels, rows, width = decayed.shape
     half = rows // 2
     mine = lax.axis_index("path") // half
-    stores = []
-    step = 0
     for send, side in ((given, 1 - mine), (kept, mine)):
         for row in range(0, half, SPAN):
             here = pl.ds(pl.multiple_of(side * half + row, SPAN), SPAN)
@@ -145,13 +140,7 @@
                 spots = places(level, here, width)
                 for chunk, at in spots:
                     first, second = moments(at, factor, grads, kept_mean, kept_square)
-                    mean[at] = first
-                    square[at] = second
                     send[row : row + SPAN, level * len(spots) + chunk, :] = stepped(first, second, decayed[at])
-                stores += write_moments(step, level, here, mean, square, new_mean, new_square, sems)
-                step += 1
-    for store in stores:
-        store.wait()
 
 
 def outer_kernel(
@@ -232,12 +221,13 @@
     )(grads[0])
     shard_count = lax.axis_size("shard")
     near = partial + lax.ppermute(partial, "shard", [(i, i ^ 1) for i in range(shard_count)])
+    clip_norm = CLIP_SHARE * math.sqrt(2 * rows * shard_count * width)
+
+    near, old_params, old_mean, old_square = lax.optimization_barrier((near, params[0], adam_mean[0], adam_square[0]))
     far = lax.ppermute(near, "shard", [(i, i ^ 2) for i in range(shard_count)])
-    clip_norm = CLIP_SHARE * math.sqrt(2 * rows * shard_count * width)
-
-    kept_mean = BETA_FIRST * adam_mean[0]
-    kept_square = BETA_SECOND * adam_square[0]
-    decayed = params[0] * (1.0 - LEARN_RATE * WEIGHT_DECAY)
+    kept_mean = BETA_FIRST * old_mean
+    kept_square = BETA_SECOND * old_square
+    decayed = old_params * (1.0 - LEARN_RATE * WEIGHT_DECAY)
     gradient = grads[0]
     staged = (decayed, kept_mean, kept_square)
     old_anchor = anchor.reshape(modules, chunks, LANES)
@@ -266,6 +256,17 @@
         )(ids, received, old_anchor, *prepared)
         return lax.all_to_all(send_back, "path", 0, 0, tiled=True), new_anchor, new_moment
 
+    def new_moments(first, second):
+        return pl.pallas_call(
+            functools.partial(moment_kernel, clip_norm),
+            out_shape=(local, local),
+            in_specs=[VMEM] * 5,
+            out_specs=(HBM, HBM),
+            scratch_shapes=[held, held, pair_sems],
+            compiler_params=grant,
+            name="moment",
+        )(near, far, gradient, first, second)
+
     def lead():
         send = pl.pallas_call(
             functools.partial(lead_kernel, clip_norm),
@@ -278,27 +279,20 @@
         received = lax.all_to_all(send, "path", 0, 0, tiled=True)
         returned, new_anchor, new_moment = update(received.reshape(rows, 1, levels * chunks, LANES))
         first, second, _ = lax.optimization_barrier((*staged[1:], returned))
-        new_mean, new_square = pl.pallas_call(
-            functools.partial(moment_kernel, clip_norm),
-            out_shape=(local, local),
-            in_specs=[VMEM] * 5,
-            out_specs=(HBM, HBM),
-            scratch_shapes=[held, held, pair_sems],
-            compiler_params=grant,
-            name="moment",
-        )(near, far, gradient, first, second)
+        new_mean, new_square = new_moments(first, second)
         return returned, new_mean, new_square, new_anchor, new_moment
 
     def follow():
-        new_mean, new_square, given, kept = pl.pallas_call(
+        new_mean, new_square = new_moments(*staged[1:])
+        first, second, _ = lax.optimization_barrier((*staged[1:], new_mean))
+        given, kept = pl.pallas_call(
             functools.partial(follow_kernel, clip_norm),
-            out_shape=(local, local, half_wire, half_wire),
+            out_shape=(half_wire, half_wire),
             in_specs=[VMEM] * 6,
-            out_specs=(HBM, HBM, VMEM, VMEM),
-            scratch_shapes=[held, held, pair_sems],
+            out_specs=(VMEM, VMEM),
             compiler_params=grant,
             name="follow",
-        )(near, far, staged[0], gradient, *staged[1:])
+        )(near, far, staged[0], gradient, first, second)
         half = paths // 2
         taken = lax.ppermute(given, "path", [(p, (p + half) % paths) for p in range(paths)])
         pair = jnp.stack([kept, taken], axis=1)

time: 81.8 us -> 81 us (level)
    all_to_all x1, blocking collectives: 26 us -> 27.4 us  [update(): lax.all_to_all(send_back, 'path', 0, 0, tiled=True)]
    all_to_all x1, blocking collectives: 30.6 us -> 29.4 us  [follow(): lax.all_to_all(pair, 'path', 0, 0, axis_index_groups=groups, tiled=True)]
    pallas_call x1 -> x2, Pallas kernels: 3.22 us -> 2.95 us  [the longest x1 1.56 us: new_moments(): pl.pallas_call(functools.partial(moment_kernel, clip_norm), out_shape=(lo...]
  transfers between devices with their start and end apart: 3 -> 3, of which waited for: 2 -> 2; matrix products, arithmetic and copies ran while one was open for 3% -> 2% of each run, Pallas kernels for 2% -> 1%
where the time goes in v4:
time: 81 us; the launch traced here: 80.8 us
  blocking collectives  56.8 us (70%)
  Pallas kernels  8.25 us (10%)
  waiting for transfers between devices  8.11 us (10%)
  starting transfers between devices  4.75 us (6%)
  other arithmetic  2.01 us (2%)
    all_to_all x1, blocking collectives, follow(): lax.all_to_all(pair, 'path', 0, 0, axis_index_groups=groups, tiled=True)  29.4 us
    all_to_all x1, blocking collectives, update(): lax.all_to_all(send_back, 'path', 0, 0, tiled=True)  27.4 us
    ppermute x1, waiting for transfers between devices, follow(): lax.ppermute(given, 'path', [(p, (p + half) % paths) for p in range(paths)])  7.16 us
    ppermute x1, starting transfers between devices, shards(): far = lax.ppermute(near, 'shard', [(i, i ^ 2) for i in range(shard_count)])  2.38 us
    ppermute x1, starting transfers between devices, follow(): lax.ppermute(given, 'path', [(p, (p + half) % paths) for p in range(paths)])  2.27 us
    mul x1, other arithmetic, shards(): decayed = old_params * (1.0 - LEARN_RATE * WEIGHT_DECAY)  1.72 us
    pallas_call x1, Pallas kernels, update(): pl.pallas_call(outer_kernel, out_shape=(owned, owned, jax.ShapeDtypeStruc...  1.62 us
  transfers between devices with their start and end apart: 3, of which 2 were waited for; matrix products, arithmetic and copies ran while one was open for 2% of the time, Pallas kernels for 1%

profile of v4, /device:TPU:8, one launch (start us, length us, event | category | flops | bytes accessed | tf_op | source)
XLA Modules:
  0.0 80.8 jit_solution(11010531987983360650)
XLA Ops:
  0.6 0.0 copy-start.4
  0.6 0.0 copy-start.5
  0.7 0.0 copy-start.6
  0.7 0.0 copy-start
  0.7 0.0 copy-start.2
  0.7 1.2 %norm.1 = f32[8,128]{1,0:T(8,128)S(1)} custom-call(bf16[2,64,2048]{2,1,0:T(8,128)(2,1)} %bitcast.17), custom_call_target="tpu_custom_call" | custom-call | tf_op jit(solution)/shard_map/norm/pallas_call | solution.py:213
  1.9 0.1 collective-permute-start.1
  2.0 0.0 copy-done.4
  2.0 0.0 copy-done.5
  2.0 0.0 copy-done.6
  2.0 0.1 pad_add_fusion.ids
  2.1 0.0 copy-done
  2.1 0.0 copy-done.2
  2.1 1.2 %prepare.1 = (f32[28,16,128]{2,1,0:T(8,128)S(1)}, f32[28,16,128]{2,1,0:T(8,128)S(1)}, f32[28,16,128]{2,1,0:T(8,128)S(1)}) custom-call(s32[192]{0:T(256)S(1)} %pad_add_fusion.ids, f32[28,16,128]{2,1,0:T(8,128)S(1)} %bitcast.20, f32[28,16,128]{2,1,0:T(8,128)S(1)} %bitcast.16), custom_call_target="tpu_custom_call" | custom-call | tf_op jit(solution)/shard_map/prepare/pallas_call | solution.py:234
  3.3 0.0 collective-permute-done.1
  3.3 0.0 copy-start.3
  3.3 2.4 %collective-permute-start.2 = (f32[8,128]{1,0:T(8,128)S(1)}, f32[8,128]{1,0:T(8,128)S(1)}, u32[]{:S(2)}, u32[]{:S(2)}) collective-permute-start(f32[8,128]{1,0:T(8,128)S(1)} %add.3), channel_id=1, source_target_pairs={{0,2},{1,3},{2,0},{3,1},{4,6},{5,7},{6,4},{7,5},{8,10},{9,11},{10,... | collective-permute-start | bytes 12296 | tf_op jit(solution)/shard_map/ppermute | solution.py:227
  5.7 1.7 %broadcast_multiply_fusion = (f32[2,64,2048]{2,1,0:T(8,128)S(1)}, f32[2,64,2048]{2,1,0:T(8,128)S(1)}) fusion(f32[2,64,2048]{2,1,0:T(8,128)} %bitcast.25, f32[2,64,2048]{2,1,0:T(8,128)} %bitcast.26), kind=kLoop, calls=%fused_computation.1 | loop fusion | flops 524288 | bytes 4194304 | tf_op jit(solution)/shard_map/mul | solution.py:230
  7.4 0.0 copy-done.3
  7.4 0.0 copy-start.1
  7.5 0.1 broadcast_multiply_fusion.2
  7.6 0.9 %collective-permute-done.2 = f32[8,128]{1,0:T(8,128)S(1)} collective-permute-done((f32[8,128]{1,0:T(8,128)S(1)}, f32[8,128]{1,0:T(8,128)S(1)}, u32[]{:S(2)}, u32[]{:S(2)}) %collective-permute-start.2) | collective-permute-done | bytes 4128 | tf_op jit(solution)/shard_map/ppermute | solution.py:227
  8.5 71.0 %conditional.1 = (f32[64,32,128]{2,1,0:T(8,128)S(1)}, f32[2,64,2048]{2,1,0:T(8,128)}, f32[2,64,2048]{2,1,0:T(8,128)}, f32[28,16,128]{2,1,0:T(8,128)}, f32[28,16,128]{2,1,0:T(8,128)}) conditional(s32[]{:T(128)} %convert_element_type.3, (f32[8,128]{1,0:T(8,128)S(1)}, f32[8,128]{1,0:T(8,128)S(1)}, bf16[2,64,2048]{2,1,0:T(8,128)(2,1)S(1)}, ...), branch_computations={%region_0.0_spmd, %region_1.0_spmd} | conditional | flops 262144 | bytes 8388688 | solution.py:305
  8.5 1.6 %moment.2 = (f32[2,64,2048]{2,1,0:T(8,128)}, f32[2,64,2048]{2,1,0:T(8,128)}) custom-call(f32[8,128]{1,0:T(8,128)S(1)} %get-tuple-element.45.near, f32[8,128]{1,0:T(8,128)S(1)} %get-tuple-element.46.far, bf16[2,64,2048]{2,1,0:T(8,128)(2,1)S(1)} %get-tuple-element.48.grads, f32[2,64,2048]{2,1,0:T(8,128)S(1)} %get-tuple-element.52.kept_mean, ...), custom_call_target="tpu_custom_call" | custom-call | tf_op jit(solution)/shard_map/cond/branch_0_fun/moment/pallas_call | solution.py:260
  10.1 1.4 %follow.1 = (f32[32,32,128]{2,1,0:T(8,128)S(1)}, f32[32,32,128]{2,1,0:T(8,128)S(1)}) custom-call(f32[8,128]{1,0:T(8,128)S(1)} %get-tuple-element.45.near, f32[8,128]{1,0:T(8,128)S(1)} %get-tuple-element.46.far, f32[2,64,2048]{2,1,0:T(8,128)S(1)} %get-tuple-element.47.decayed, bf16[2,64,2048]{2,1,0:T(8,128)(2,1)S(1)} %get-tuple-element.48.grads, ...), custom_call_target="tpu_custom_call" | custom-call | tf_op jit(solution)/shard_map/cond/branch_0_fun/follow/pallas_call | solution.py:288
  11.5 2.3 %collective-permute-start = (f32[32,32,128]{2,1,0:T(8,128)S(1)}, f32[32,32,128]{2,1,0:T(8,128)S(1)}, u32[]{:S(2)}, u32[]{:S(2)}) collective-permute-start(f32[32,32,128]{2,1,0:T(8,128)S(1)} %get-tuple-element.55), channel_id=1, source_target_pairs={{0,128},{4,132},{8,136},{12,140},{16,144},{20,148},{24,152},{28,15... | collective-permute-start | bytes 1572872 | tf_op jit(solution)/shard_map/cond/branch_0_fun/ppermute | solution.py:297
  13.8 7.2 %collective-permute-done = f32[32,32,128]{2,1,0:T(8,128)S(1)} collective-permute-done((f32[32,32,128]{2,1,0:T(8,128)S(1)}, f32[32,32,128]{2,1,0:T(8,128)S(1)}, u32[]{:S(2)}, u32[]{:S(2)}) %collective-permute-start) | collective-permute-done | bytes 524320 | tf_op jit(solution)/shard_map/cond/branch_0_fun/ppermute | solution.py:297
  20.9 0.1 pad_maximum_fusion
  21.0 29.4 %all_to_all.16.received = f32[32,2,32,128]{3,2,1,0:T(8,128)S(1)} all-to-all(f32[32,2,32,128]{3,2,1,0:T(8,128)S(1)} %pad_maximum_fusion), channel_id=1, replica_groups={{0,4,8,12,16,20,24,28,32,36,40,44,48,52,56,60,64,68,72,76,80,84,88,92,9..., dimensions={0} | all-to-all | bytes 2097152 | tf_op jit(solution)/shard_map/cond/branch_0_fun/all_to_all | solution.py:300
  50.4 1.6 %outer.2 = (f32[28,16,128]{2,1,0:T(8,128)}, f32[28,16,128]{2,1,0:T(8,128)}, f32[64,32,128]{2,1,0:T(8,128)S(1)}) custom-call(s32[192]{0:T(256)S(1)} %get-tuple-element.44.ids, f32[32,2,32,128]{3,2,1,0:T(8,128)S(1)} %all_to_all.16.received, f32[28,16,128]{2,1,0:T(8,128)S(1)} %get-tuple-element.56.anchor, f32[28,16,128]{2,1,0:T(8,128)S(1)} %get-tuple-element.57.scaled, ...), custom_call_target="tpu_custom_call" | custom-call | tf_op jit(solution)/shard_map/cond/branch_0_fun/outer/pallas_call | solution.py:246
  52.1 27.4 %all_to_all.17 = f32[64,32,128]{2,1,0:T(8,128)S(1)} all-to-all(f32[64,32,128]{2,1,0:T(8,128)S(1)} %get-tuple-element.60), channel_id=1, replica_groups=mesh['path'=64,'shard'=4] {'path'}, dimensions={0} | all-to-all | bytes 2097152 | tf_op jit(solution)/shard_map/cond/branch_0_fun/all_to_all | solution.py:257
  79.5 1.3 %place.1 = f32[2,64,2048]{2,1,0:T(8,128)} custom-call(f32[64,32,128]{2,1,0:T(8,128)S(1)} %get-tuple-element.106.received), custom_call_target="tpu_custom_call" | custom-call | tf_op jit(solution)/shard_map/place/pallas_call | solution.py:306
  (2 shorter events, 0.0 us)
Async XLA Ops:
  0.6 1.4 %copy-start.4 = (s32[64]{0:T(128)S(1)}, s32[64]{0:T(128)}, u32[]{:S(2)}) copy-start(s32[64]{0:T(128)} %param.19) | copy-start | bytes 772
  0.6 1.4 %copy-start.5 = (s32[64]{0:T(128)S(1)}, s32[64]{0:T(128)}, u32[]{:S(2)}) copy-start(s32[64]{0:T(128)} %param.18) | copy-start | bytes 772
  0.7 1.4 %copy-start.6 = (s32[64]{0:T(128)S(1)}, s32[64]{0:T(128)}, u32[]{:S(2)}) copy-start(s32[64]{0:T(128)} %param.17) | copy-start | bytes 772
  0.7 1.4 %copy-start = (f32[28,1,2048]{2,1,0:T(1,128)S(1)}, f32[28,1,2048]{2,1,0:T(1,128)}, u32[]{:S(2)}) copy-start(f32[28,1,2048]{2,1,0:T(1,128)} %param.16) | copy-start | bytes 688132
  0.7 1.4 %copy-start.2 = (f32[28,1,2048]{2,1,0:T(1,128)S(1)}, f32[28,1,2048]{2,1,0:T(1,128)}, u32[]{:S(2)}) copy-start(f32[28,1,2048]{2,1,0:T(1,128)} %param.15) | copy-start | bytes 688132
  1.9 1.4 %collective-permute-start.1 = (f32[8,128]{1,0:T(8,128)S(1)}, f32[8,128]{1,0:T(8,128)S(1)}, u32[]{:S(2)}, u32[]{:S(2)}) collective-permute-start(f32[8,128]{1,0:T(8,128)S(1)} %norm.1), channel_id=1, source_target_pairs={{0,1},{1,0},{2,3},{3,2},{4,5},{5,4},{6,7},{7,6},{8,9},{9,8},{10,11... | collective-permute-start | bytes 12296 | tf_op jit(solution)/shard_map/ppermute | solution.py:223
  3.3 4.1 %copy-start.3 = (f32[1,2,64,2048]{3,2,1,0:T(8,128)S(1)}, f32[1,2,64,2048]{3,2,1,0:T(8,128)}, u32[]{:S(2)}) copy-start(f32[1,2,64,2048]{3,2,1,0:T(8,128)} %param.13) | copy-start | bytes 3145732
  3.3 5.2 %collective-permute-start.2 = (f32[8,128]{1,0:T(8,128)S(1)}, f32[8,128]{1,0:T(8,128)S(1)}, u32[]{:S(2)}, u32[]{:S(2)}) collective-permute-start(f32[8,128]{1,0:T(8,128)S(1)} %add.3), channel_id=1, source_target_pairs={{0,2},{1,3},{2,0},{3,1},{4,6},{5,7},{6,4},{7,5},{8,10},{9,11},{10,... | collective-permute-start | bytes 12296 | tf_op jit(solution)/shard_map/ppermute | solution.py:227
  7.4 1.1 %copy-start.1 = (bf16[1,2,64,2048]{3,2,1,0:T(8,128)(2,1)S(1)}, bf16[1,2,64,2048]{3,2,1,0:T(8,128)(2,1)}, u32[]{:S(2)}) copy-start(bf16[1,2,64,2048]{3,2,1,0:T(8,128)(2,1)} %param.12) | copy-start | bytes 1572868
  11.5 9.4 %collective-permute-start = (f32[32,32,128]{2,1,0:T(8,128)S(1)}, f32[32,32,128]{2,1,0:T(8,128)S(1)}, u32[]{:S(2)}, u32[]{:S(2)}) collective-permute-start(f32[32,32,128]{2,1,0:T(8,128)S(1)} %get-tuple-element.55), channel_id=1, source_target_pairs={{0,128},{4,132},{8,136},{12,140},{16,144},{20,148},{24,152},{28,15... | collective-permute-start | bytes 1572872 | tf_op jit(solution)/shard_map/cond/branch_0_fun/ppermute | solution.py:297

commit v5 on v4

--- a/solution.py
+++ b/solution.py
@@ -144,18 +144,26 @@
 
 
 def outer_kernel(
-    ids, received, anchor, scaled, inverse, kept_moment, new_anchor, new_moment, send,
-    anchor_held, moment_held, sems, *sums,
+    prepared, ids, received, anchor, *refs,
 ):
+    given, (new_anchor, new_moment, send, anchor_held, moment_held, totals, sems, *sums) = (
+        (refs[:3], refs[3:]) if prepared else (refs[:1], refs[1:])
+    )
     paths = ids.shape[0] // 3
     rows = received.shape[0]
     modules, chunks, _ = anchor.shape
     first_side = lax.axis_index("path") // rows if rows < paths else 0
     for each in sums:
         each[...] = jnp.zeros_like(each)
+    for module in range(0 if prepared else modules):
+        totals[module] = 0
     for path in range(paths):
         lane = path % LANES_OF_SUMS
-        weight = jnp.full((chunks, LANES), ids[2 * paths + path], jnp.int32).astype(jnp.float32)
+        count = ids[2 * paths + path]
+        if not prepared:
+            totals[ids[path]] += count
+            totals[ids[paths + path] + LOW] += count
+        weight = jnp.full((chunks, LANES), count, jnp.int32).astype(jnp.float32)
         side, row = divmod(path, rows)
         slot = side ^ first_side
         sums[lane][ids[path]] += weight * received[row, slot, :chunks, :]
@@ -163,8 +171,14 @@
     for module in range(modules):
         start, place = (0, module) if module < LOW else (LANES_OF_SUMS, module - LOW)
         summed = sum(sums[start + lane][place] for lane in range(LANES_OF_SUMS))
-        outer_grad = (scaled[module] - summed) * inverse[module]
-        moment = kept_moment[module] + outer_grad
+        if prepared:
+            scaled, inverse, kept_moment = (ref[module] for ref in given)
+        else:
+            total = jnp.full((chunks, LANES), totals[module], jnp.int32).astype(jnp.float32)
+            scaled, inverse = total * anchor[module], 1.0 / jnp.maximum(total, 1.0)
+            kept_moment = OUTER_MOMENTUM * given[0][module]
+        outer_grad = (scaled - summed) * inverse
+        moment = kept_moment + outer_grad
         moment_held[module] = moment
         anchor_held[module] = anchor[module] - OUTER_RATE * (outer_grad + OUTER_MOMENTUM * moment)
     stores = [
@@ -231,29 +245,21 @@
     gradient = grads[0]
     staged = (decayed, kept_mean, kept_square)
     old_anchor = anchor.reshape(modules, chunks, LANES)
-    prepared = pl.pallas_call(
-        prepare_kernel,
-        out_shape=(owned,) * 3,
-        in_specs=[SMEM] + [VMEM] * 2,
-        out_specs=(VMEM,) * 3,
-        scratch_shapes=[pltpu.SMEM((modules,), jnp.int32)],
-        compiler_params=grant,
-        name="prepare",
-    )(ids, old_anchor, momentum.reshape(modules, chunks, LANES))
-    prepared = lax.optimization_barrier(prepared)
-
-    def update(received):
+    old_momentum = momentum.reshape(modules, chunks, LANES)
+
+    def update(received, prepared, *given):
         new_anchor, new_moment, send_back = pl.pallas_call(
-            outer_kernel,
+            functools.partial(outer_kernel, prepared),
             out_shape=(owned, owned, jax.ShapeDtypeStruct((paths, levels * chunks, LANES), f32)),
-            in_specs=[SMEM] + [VMEM] * 5,
+            in_specs=[SMEM] + [VMEM] * (2 + len(given)),
             out_specs=(HBM, HBM, VMEM),
-            scratch_shapes=[pltpu.VMEM((modules, chunks, LANES), f32)] * 2 + [pltpu.SemaphoreType.DMA((2,))]
+            scratch_shapes=[pltpu.VMEM((modules, chunks, LANES), f32)] * 2
+            + [pltpu.SMEM((modules,), jnp.int32), pltpu.SemaphoreType.DMA((2,))]
             + [pltpu.VMEM((LOW, chunks, LANES), f32)] * LANES_OF_SUMS
             + [pltpu.VMEM((modules - LOW, chunks, LANES), f32)] * LANES_OF_SUMS,
             compiler_params=grant,
             name="outer",
-        )(ids, received, old_anchor, *prepared)
+        )(ids, received, old_anchor, *given)
         return lax.all_to_all(send_back, "path", 0, 0, tiled=True), new_anchor, new_moment
 
     def new_moments(first, second):
@@ -277,7 +283,9 @@
             name="lead",
         )(near, far, staged[0], gradient, *staged[1:])
         received = lax.all_to_all(send, "path", 0, 0, tiled=True)
-        returned, new_anchor, new_moment = update(received.reshape(rows, 1, levels * chunks, LANES))
+        returned, new_anchor, new_moment = update(
+            received.reshape(rows, 1, levels * chunks, LANES), False, old_momentum
+        )
         first, second, _ = lax.optimization_barrier((*staged[1:], returned))
         new_mean, new_square = new_moments(first, second)
         return returned, new_mean, new_square, new_anchor, new_moment
@@ -293,12 +301,22 @@
             compiler_params=grant,
             name="follow",
         )(near, far, staged[0], gradient, first, second)
+        prepared = pl.pallas_call(
+            prepare_kernel,
+            out_shape=(owned,) * 3,
+            in_specs=[SMEM] + [VMEM] * 2,
+            out_specs=(VMEM,) * 3,
+            scratch_shapes=[pltpu.SMEM((modules,), jnp.int32)],
+            compiler_params=grant,
+            name="prepare",
+        )(*lax.optimization_barrier((ids, old_anchor, old_momentum, given))[:3])
         half = paths // 2
         taken = lax.ppermute(given, "path", [(p, (p + half) % paths) for p in range(paths)])
+        taken, prepared = lax.optimization_barrier((taken, prepared))
         pair = jnp.stack([kept, taken], axis=1)
         groups = [list(range(half)), list(range(half, paths))]
         received = lax.all_to_all(pair, "path", 0, 0, axis_index_groups=groups, tiled=True)
-        returned, new_anchor, new_moment = update(received)
+        returned, new_anchor, new_moment = update(received, True, *prepared)
         return returned, new_mean, new_square, new_anchor, new_moment
 
     leads = lax.rem(lax.axis_index("shard"), 2) == 1

time: 81 us -> 80.5 us (level)
    all_to_all x1, blocking collectives: 27.4 us -> 26.1 us  [update(): lax.all_to_all(send_back, 'path', 0, 0, tiled=True)]
    ppermute x1, waiting for transfers between devices: 7.16 us -> 5.98 us  [follow(): lax.ppermute(given, 'path', [(p, (p + half) % paths) for p in range(paths)])]
    all_to_all x1, blocking collectives: 29.4 us -> 30.5 us  [follow(): lax.all_to_all(pair, 'path', 0, 0, axis_index_groups=groups, tiled=True)]
    ppermute x1, waiting for transfers between devices: 0.01 us -> 1.05 us  [shards(): lax.ppermute(partial, 'shard', [(i, i ^ 1) for i in range(shard_count)])]
  transfers between devices with their start and end apart: 3 -> 3, of which waited for: 2 -> 3; matrix products, arithmetic and copies ran while one was open for 2% -> 2% of each run, Pallas kernels for 1% -> 1%
where the time goes in v5:
time: 80.5 us; the launch traced here: 80.1 us
  blocking collectives  56.5 us (70%)
  Pallas kernels  8.15 us (10%)
  waiting for transfers between devices  7.9 us (10%)
  starting transfers between devices  4.53 us (6%)
  other arithmetic  2.04 us (3%)
    all_to_all x1, blocking collectives, follow(): lax.all_to_all(pair, 'path', 0, 0, axis_index_groups=groups, tiled=True)  30.5 us
    all_to_all x1, blocking collectives, update(): lax.all_to_all(send_back, 'path', 0, 0, tiled=True)  26.1 us
    ppermute x1, waiting for transfers between devices, follow(): lax.ppermute(given, 'path', [(p, (p + half) % paths) for p in range(paths)])  5.98 us
    ppermute x1, starting transfers between devices, shards(): far = lax.ppermute(near, 'shard', [(i, i ^ 2) for i in range(shard_count)])  2.3 us
    ppermute x1, starting transfers between devices, follow(): lax.ppermute(given, 'path', [(p, (p + half) % paths) for p in range(paths)])  2.15 us
    mul x1, other arithmetic, shards(): decayed = old_params * (1.0 - LEARN_RATE * WEIGHT_DECAY)  1.78 us
    pallas_call x1, Pallas kernels, update(): pl.pallas_call(functools.partial(outer_kernel, prepared), out_shape=(owne...  1.61 us
  transfers between devices with their start and end apart: 3, of which 3 were waited for; matrix products, arithmetic and copies ran while one was open for 2% of the time, Pallas kernels for 1%

profile of v5, /device:TPU:8, one launch (start us, length us, event | category | flops | bytes accessed | tf_op | source)
XLA Modules:
  0.0 80.1 jit_solution(14286916683648431559)
XLA Ops:
  0.6 0.0 copy-start.4
  0.6 0.0 copy-start.5
  0.7 0.0 copy-start.6
  0.7 1.2 %norm.1 = f32[8,128]{1,0:T(8,128)S(1)} custom-call(bf16[2,64,2048]{2,1,0:T(8,128)(2,1)} %bitcast.16), custom_call_target="tpu_custom_call" | custom-call | tf_op jit(solution)/shard_map/norm/pallas_call | solution.py:227
  1.8 0.1 collective-permute-start.1
  1.9 0.0 copy-done.4
  1.9 0.0 copy-done.5
  2.0 0.0 copy-done.6
  2.0 0.1 pad_add_fusion
  2.0 1.0 %collective-permute-done.1 = f32[8,128]{1,0:T(8,128)S(1)} collective-permute-done((f32[8,128]{1,0:T(8,128)S(1)}, f32[8,128]{1,0:T(8,128)S(1)}, u32[]{:S(2)}, u32[]{:S(2)}) %collective-permute-start.1) | collective-permute-done | bytes 4128 | tf_op jit(solution)/shard_map/ppermute | solution.py:237
  3.1 2.3 %collective-permute-start.2 = (f32[8,128]{1,0:T(8,128)S(1)}, f32[8,128]{1,0:T(8,128)S(1)}, u32[]{:S(2)}, u32[]{:S(2)}) collective-permute-start(f32[8,128]{1,0:T(8,128)S(1)} %add.3), channel_id=1, source_target_pairs={{0,2},{1,3},{2,0},{3,1},{4,6},{5,7},{6,4},{7,5},{8,10},{9,11},{10,... | collective-permute-start | bytes 12296 | tf_op jit(solution)/shard_map/ppermute | solution.py:241
  5.4 1.8 %broadcast_multiply_fusion = (f32[2,64,2048]{2,1,0:T(8,128)S(1)}, f32[2,64,2048]{2,1,0:T(8,128)S(1)}) fusion(f32[2,64,2048]{2,1,0:T(8,128)} %bitcast.23, f32[2,64,2048]{2,1,0:T(8,128)} %bitcast.24), kind=kLoop, calls=%fused_computation.1 | loop fusion | flops 524288 | bytes 4194304 | tf_op jit(solution)/shard_map/mul | solution.py:244
  7.2 0.0 copy-done.2
  7.2 0.0 copy-start
  7.2 0.0 copy-start.1
  7.2 0.0 copy-start.3
  7.2 0.1 broadcast_multiply_fusion.2
  7.3 0.9 %collective-permute-done.2 = f32[8,128]{1,0:T(8,128)S(1)} collective-permute-done((f32[8,128]{1,0:T(8,128)S(1)}, f32[8,128]{1,0:T(8,128)S(1)}, u32[]{:S(2)}, u32[]{:S(2)}) %collective-permute-start.2) | collective-permute-done | bytes 4128 | tf_op jit(solution)/shard_map/ppermute | solution.py:241
  8.2 0.0 copy-done
  8.2 0.1 copy-done.1
  8.3 0.1 copy-done.3
  8.4 70.5 %conditional.1 = (f32[64,32,128]{2,1,0:T(8,128)S(1)}, f32[2,64,2048]{2,1,0:T(8,128)}, f32[2,64,2048]{2,1,0:T(8,128)}, f32[28,16,128]{2,1,0:T(8,128)}, f32[28,16,128]{2,1,0:T(8,128)}) conditional(s32[]{:T(128)} %convert_element_type.3, (f32[8,128]{1,0:T(8,128)S(1)}, f32[8,128]{1,0:T(8,128)S(1)}, bf16[2,64,2048]{2,1,0:T(8,128)(2,1)S(1)}, ...), branch_computations={%region_0.0_spmd, %region_1.0_spmd} | conditional | flops 262144 | bytes 8388688 | solution.py:323
  8.4 1.6 %moment.2 = (f32[2,64,2048]{2,1,0:T(8,128)}, f32[2,64,2048]{2,1,0:T(8,128)}) custom-call(f32[8,128]{1,0:T(8,128)S(1)} %get-tuple-element.37.near, f32[8,128]{1,0:T(8,128)S(1)} %get-tuple-element.38.far, bf16[2,64,2048]{2,1,0:T(8,128)(2,1)S(1)} %get-tuple-element.40.grads, f32[2,64,2048]{2,1,0:T(8,128)S(1)} %get-tuple-element.44.kept_mean, ...), custom_call_target="tpu_custom_call" | custom-call | tf_op jit(solution)/shard_map/cond/branch_0_fun/moment/pallas_call | solution.py:266
  9.9 1.4 %follow.1 = (f32[32,32,128]{2,1,0:T(8,128)S(1)}, f32[32,32,128]{2,1,0:T(8,128)S(1)}) custom-call(f32[8,128]{1,0:T(8,128)S(1)} %get-tuple-element.37.near, f32[8,128]{1,0:T(8,128)S(1)} %get-tuple-element.38.far, f32[2,64,2048]{2,1,0:T(8,128)S(1)} %get-tuple-element.39.decayed, bf16[2,64,2048]{2,1,0:T(8,128)(2,1)S(1)} %get-tuple-element.40.grads, ...), custom_call_target="tpu_custom_call" | custom-call | tf_op jit(solution)/shard_map/cond/branch_0_fun/follow/pallas_call | solution.py:296
  11.3 2.1 %collective-permute-start = (f32[32,32,128]{2,1,0:T(8,128)S(1)}, f32[32,32,128]{2,1,0:T(8,128)S(1)}, u32[]{:S(2)}, u32[]{:S(2)}) collective-permute-start(f32[32,32,128]{2,1,0:T(8,128)S(1)} %get-tuple-element.47), channel_id=1, source_target_pairs={{0,128},{4,132},{8,136},{12,140},{16,144},{20,148},{24,152},{28,15... | collective-permute-start | bytes 1572872 | tf_op jit(solution)/shard_map/cond/branch_0_fun/ppermute | solution.py:314
  13.4 1.2 %prepare.1 = (f32[28,16,128]{2,1,0:T(8,128)S(1)}, f32[28,16,128]{2,1,0:T(8,128)S(1)}, f32[28,16,128]{2,1,0:T(8,128)S(1)}) custom-call(s32[192]{0:T(256)S(1)} %get-tuple-element.50.ids, f32[28,16,128]{2,1,0:T(8,128)S(1)} %get-tuple-element.51.anchor, f32[28,16,128]{2,1,0:T(8,128)S(1)} %get-tuple-element.52.momentum), custom_call_target="tpu_custom_call" | custom-call | tf_op jit(solution)/shard_map/cond/branch_0_fun/prepare/pallas_call | solution.py:304
  14.6 6.0 %collective-permute-done = f32[32,32,128]{2,1,0:T(8,128)S(1)} collective-permute-done((f32[32,32,128]{2,1,0:T(8,128)S(1)}, f32[32,32,128]{2,1,0:T(8,128)S(1)}, u32[]{:S(2)}, u32[]{:S(2)}) %collective-permute-start) | collective-permute-done | bytes 524320 | tf_op jit(solution)/shard_map/cond/branch_0_fun/ppermute | solution.py:314
  20.6 0.1 pad_maximum_fusion
  20.7 30.5 %all_to_all.16.received = f32[32,2,32,128]{3,2,1,0:T(8,128)S(1)} all-to-all(f32[32,2,32,128]{3,2,1,0:T(8,128)S(1)} %pad_maximum_fusion), channel_id=1, replica_groups={{0,4,8,12,16,20,24,28,32,36,40,44,48,52,56,60,64,68,72,76,80,84,88,92,9..., dimensions={0} | all-to-all | bytes 2097152 | tf_op jit(solution)/shard_map/cond/branch_0_fun/all_to_all | solution.py:318
  51.2 1.6 %outer.2 = (f32[28,16,128]{2,1,0:T(8,128)}, f32[28,16,128]{2,1,0:T(8,128)}, f32[64,32,128]{2,1,0:T(8,128)S(1)}) custom-call(s32[192]{0:T(256)S(1)} %get-tuple-element.50.ids, f32[32,2,32,128]{3,2,1,0:T(8,128)S(1)} %all_to_all.16.received, f32[28,16,128]{2,1,0:T(8,128)S(1)} %get-tuple-element.51.anchor, f32[28,16,128]{2,1,0:T(8,128)S(1)} %get-tuple-element.57.refs_0_, ...), custom_call_target="tpu_custom_call" | custom-call | tf_op jit(solution)/shard_map/cond/branch_0_fun/outer/pallas_call | solution.py:251
  52.8 26.1 %all_to_all.17 = f32[64,32,128]{2,1,0:T(8,128)S(1)} all-to-all(f32[64,32,128]{2,1,0:T(8,128)S(1)} %get-tuple-element.60), channel_id=1, replica_groups=mesh['path'=64,'shard'=4] {'path'}, dimensions={0} | all-to-all | bytes 2097152 | tf_op jit(solution)/shard_map/cond/branch_0_fun/all_to_all | solution.py:263
  78.8 1.3 %place.1 = f32[2,64,2048]{2,1,0:T(8,128)} custom-call(f32[64,32,128]{2,1,0:T(8,128)S(1)} %get-tuple-element.98.received), custom_call_target="tpu_custom_call" | custom-call | tf_op jit(solution)/shard_map/place/pallas_call | solution.py:324
  (2 shorter events, 0.0 us)
Async XLA Ops:
  0.6 1.3 %copy-start.4 = (s32[64]{0:T(128)S(1)}, s32[64]{0:T(128)}, u32[]{:S(2)}) copy-start(s32[64]{0:T(128)} %param.19) | copy-start | bytes 772
  0.6 1.3 %copy-start.5 = (s32[64]{0:T(128)S(1)}, s32[64]{0:T(128)}, u32[]{:S(2)}) copy-start(s32[64]{0:T(128)} %param.18) | copy-start | bytes 772
  0.7 1.3 %copy-start.6 = (s32[64]{0:T(128)S(1)}, s32[64]{0:T(128)}, u32[]{:S(2)}) copy-start(s32[64]{0:T(128)} %param.17) | copy-start | bytes 772
  1.8 1.3 %collective-permute-start.1 = (f32[8,128]{1,0:T(8,128)S(1)}, f32[8,128]{1,0:T(8,128)S(1)}, u32[]{:S(2)}, u32[]{:S(2)}) collective-permute-start(f32[8,128]{1,0:T(8,128)S(1)} %norm.1), channel_id=1, source_target_pairs={{0,1},{1,0},{2,3},{3,2},{4,5},{5,4},{6,7},{7,6},{8,9},{9,8},{10,11... | collective-permute-start | bytes 12296 | tf_op jit(solution)/shard_map/ppermute | solution.py:237
  3.1 4.1 %copy-start.2 = (f32[1,2,64,2048]{3,2,1,0:T(8,128)S(1)}, f32[1,2,64,2048]{3,2,1,0:T(8,128)}, u32[]{:S(2)}) copy-start(f32[1,2,64,2048]{3,2,1,0:T(8,128)} %param.13) | copy-start | bytes 3145732
  3.1 5.1 %collective-permute-start.2 = (f32[8,128]{1,0:T(8,128)S(1)}, f32[8,128]{1,0:T(8,128)S(1)}, u32[]{:S(2)}, u32[]{:S(2)}) collective-permute-start(f32[8,128]{1,0:T(8,128)S(1)} %add.3), channel_id=1, source_target_pairs={{0,2},{1,3},{2,0},{3,1},{4,6},{5,7},{6,4},{7,5},{8,10},{9,11},{10,... | collective-permute-start | bytes 12296 | tf_op jit(solution)/shard_map/ppermute | solution.py:241
  7.2 1.0 %copy-start = (bf16[1,2,64,2048]{3,2,1,0:T(8,128)(2,1)S(1)}, bf16[1,2,64,2048]{3,2,1,0:T(8,128)(2,1)}, u32[]{:S(2)}) copy-start(bf16[1,2,64,2048]{3,2,1,0:T(8,128)(2,1)} %param.12) | copy-start | bytes 1572868
  7.2 1.1 %copy-start.1 = (f32[28,1,2048]{2,1,0:T(1,128)S(1)}, f32[28,1,2048]{2,1,0:T(1,128)}, u32[]{:S(2)}) copy-start(f32[28,1,2048]{2,1,0:T(1,128)} %param.15) | copy-start | bytes 688132
  7.2 1.1 %copy-start.3 = (f32[28,1,2048]{2,1,0:T(1,128)S(1)}, f32[28,1,2048]{2,1,0:T(1,128)}, u32[]{:S(2)}) copy-start(f32[28,1,2048]{2,1,0:T(1,128)} %param.16) | copy-start | bytes 688132
  11.3 9.3 %collective-permute-start = (f32[32,32,128]{2,1,0:T(8,128)S(1)}, f32[32,32,128]{2,1,0:T(8,128)S(1)}, u32[]{:S(2)}, u32[]{:S(2)}) collective-permute-start(f32[32,32,128]{2,1,0:T(8,128)S(1)} %get-tuple-element.47), channel_id=1, source_target_pairs={{0,128},{4,132},{8,136},{12,140},{16,144},{20,148},{24,152},{28,15... | collective-permute-start | bytes 1572872 | tf_op jit(solution)/shard_map/cond/branch_0_fun/ppermute | solution.py:314

commit v6 on v5

--- a/solution.py
+++ b/solution.py
@@ -237,11 +237,11 @@
     near = partial + lax.ppermute(partial, "shard", [(i, i ^ 1) for i in range(shard_count)])
     clip_norm = CLIP_SHARE * math.sqrt(2 * rows * shard_count * width)
 
-    near, old_params, old_mean, old_square = lax.optimization_barrier((near, params[0], adam_mean[0], adam_square[0]))
+    near, old_mean, old_square = lax.optimization_barrier((near, adam_mean[0], adam_square[0]))
     far = lax.ppermute(near, "shard", [(i, i ^ 2) for i in range(shard_count)])
     kept_mean = BETA_FIRST * old_mean
     kept_square = BETA_SECOND * old_square
-    decayed = old_params * (1.0 - LEARN_RATE * WEIGHT_DECAY)
+    decayed = params[0] * (1.0 - LEARN_RATE * WEIGHT_DECAY)
     gradient = grads[0]
     staged = (decayed, kept_mean, kept_square)
     old_anchor = anchor.reshape(modules, chunks, LANES)

time: 80.5 us -> 82 us (1.019)
    ppermute x1, waiting for transfers between devices: 0.88 us -> 2.61 us  [shards(): far = lax.ppermute(near, 'shard', [(i, i ^ 2) for i in range(shard_count)])]
    all_to_all x1, blocking collectives: 26.1 us -> 27.3 us  [update(): lax.all_to_all(send_back, 'path', 0, 0, tiled=True)]
    all_to_all x1, blocking collectives: 30.5 us -> 29.3 us  [follow(): lax.all_to_all(pair, 'path', 0, 0, axis_index_groups=groups, tiled=True)]
    ppermute x1, waiting for transfers between devices: 1.05 us -> 0.01 us  [shards(): lax.ppermute(partial, 'shard', [(i, i ^ 1) for i in range(shard_count)])]
  transfers between devices with their start and end apart: 3 -> 3, of which waited for: 3 -> 2; matrix products, arithmetic and copies ran while one was open for 2% -> 3% of each run, Pallas kernels for 1% -> 1%
where the time goes in v6:
time: 82 us; the launch traced here: 81.8 us
  blocking collectives  56.6 us (69%)
  waiting for transfers between devices  8.59 us (10%)
  Pallas kernels  8.18 us (10%)
  starting transfers between devices  4.76 us (6%)
  other arithmetic  2.79 us (3%)
    all_to_all x1, blocking collectives, follow(): lax.all_to_all(pair, 'path', 0, 0, axis_index_groups=groups, tiled=True)  29.3 us
    all_to_all x1, blocking collectives, update(): lax.all_to_all(send_back, 'path', 0, 0, tiled=True)  27.3 us
    ppermute x1, waiting for transfers between devices, follow(): lax.ppermute(given, 'path', [(p, (p + half) % paths) for p in range(paths)])  5.98 us
    ppermute x1, waiting for transfers between devices, shards(): far = lax.ppermute(near, 'shard', [(i, i ^ 2) for i in range(shard_count)])  2.61 us
    mul x1, other arithmetic, shards(): decayed = params[0] * (1.0 - LEARN_RATE * WEIGHT_DECAY)  2.43 us
    ppermute x1, starting transfers between devices, shards(): far = lax.ppermute(near, 'shard', [(i, i ^ 2) for i in range(shard_count)])  2.4 us
    ppermute x1, starting transfers between devices, follow(): lax.ppermute(given, 'path', [(p, (p + half) % paths) for p in range(paths)])  2.27 us
  transfers between devices with their start and end apart: 3, of which 2 were waited for; matrix products, arithmetic and copies ran while one was open for 3% of the time, Pallas kernels for 1%

profile of v6, /device:TPU:8, one launch (start us, length us, event | category | flops | bytes accessed | tf_op | source)
XLA Modules:
  0.0 81.8 jit_solution(14687141163077609261)
XLA Ops:
  0.6 0.0 copy-start.6
  0.6 0.0 copy-start.7
  0.7 0.0 copy-start.8
  0.7 1.2 %norm.1 = f32[8,128]{1,0:T(8,128)S(1)} custom-call(bf16[2,64,2048]{2,1,0:T(8,128)(2,1)} %bitcast.17), custom_call_target="tpu_custom_call" | custom-call | tf_op jit(solution)/shard_map/norm/pallas_call | solution.py:227
  1.8 0.0 copy-start.3
  1.8 0.0 copy-start.4
  1.9 0.1 collective-permute-start.1
  2.0 2.4 %multiply_bitcast_fusion = f32[2,64,2048]{2,1,0:T(8,128)} fusion(f32[1,2,64,2048]{3,2,1,0:T(8,128)} %param.11), kind=kLoop, calls=%fused_computation.1 | loop fusion | flops 262144 | bytes 2097152 | tf_op jit(solution)/shard_map/mul | solution.py:244
  4.4 0.0 copy-done.6
  4.4 0.0 copy-done.7
  4.4 0.0 copy-done.8
  4.4 0.1 pad_add_fusion
  4.5 0.0 collective-permute-done.1
  4.5 0.0 copy-start.1
  4.5 0.0 copy-start.2
  4.5 0.0 copy-start.5
  4.5 2.4 %collective-permute-start.2 = (f32[8,128]{1,0:T(8,128)S(1)}, f32[8,128]{1,0:T(8,128)S(1)}, u32[]{:S(2)}, u32[]{:S(2)}) collective-permute-start(f32[8,128]{1,0:T(8,128)S(1)} %add.3), channel_id=1, source_target_pairs={{0,2},{1,3},{2,0},{3,1},{4,6},{5,7},{6,4},{7,5},{8,10},{9,11},{10,... | collective-permute-start | bytes 12296 | tf_op jit(solution)/shard_map/ppermute | solution.py:241
  6.9 0.0 copy-done.3
  6.9 0.2 broadcast_multiply_fusion
  7.1 2.6 %collective-permute-done.2 = f32[8,128]{1,0:T(8,128)S(1)} collective-permute-done((f32[8,128]{1,0:T(8,128)S(1)}, f32[8,128]{1,0:T(8,128)S(1)}, u32[]{:S(2)}, u32[]{:S(2)}) %collective-permute-start.2) | collective-permute-done | bytes 4128 | tf_op jit(solution)/shard_map/ppermute | solution.py:241
  9.7 0.0 copy-done.1
  9.8 70.8 %conditional.1 = (f32[64,32,128]{2,1,0:T(8,128)S(1)}, f32[2,64,2048]{2,1,0:T(8,128)}, f32[2,64,2048]{2,1,0:T(8,128)}, f32[28,16,128]{2,1,0:T(8,128)}, f32[28,16,128]{2,1,0:T(8,128)}) conditional(s32[]{:T(128)} %convert_element_type.3, (f32[8,128]{1,0:T(8,128)S(1)}, f32[8,128]{1,0:T(8,128)S(1)}, bf16[2,64,2048]{2,1,0:T(8,128)(2,1)S(1)}, ...), branch_computations={%region_0.0_spmd, %region_1.0_spmd} | conditional | flops 262144 | bytes 8388688 | solution.py:323
  9.8 1.6 %moment.2 = (f32[2,64,2048]{2,1,0:T(8,128)}, f32[2,64,2048]{2,1,0:T(8,128)}) custom-call(f32[8,128]{1,0:T(8,128)S(1)} %get-tuple-element.37.near, f32[8,128]{1,0:T(8,128)S(1)} %get-tuple-element.38.far, bf16[2,64,2048]{2,1,0:T(8,128)(2,1)S(1)} %get-tuple-element.40.grads, f32[2,64,2048]{2,1,0:T(8,128)S(1)} %get-tuple-element.44.kept_mean, ...), custom_call_target="tpu_custom_call" | custom-call | tf_op jit(solution)/shard_map/cond/branch_0_fun/moment/pallas_call | solution.py:266
  11.3 1.4 %follow.1 = (f32[32,32,128]{2,1,0:T(8,128)S(1)}, f32[32,32,128]{2,1,0:T(8,128)S(1)}) custom-call(f32[8,128]{1,0:T(8,128)S(1)} %get-tuple-element.37.near, f32[8,128]{1,0:T(8,128)S(1)} %get-tuple-element.38.far, f32[2,64,2048]{2,1,0:T(8,128)S(1)} %get-tuple-element.39.decayed, bf16[2,64,2048]{2,1,0:T(8,128)(2,1)S(1)} %get-tuple-element.40.grads, ...), custom_call_target="tpu_custom_call" | custom-call | tf_op jit(solution)/shard_map/cond/branch_0_fun/follow/pallas_call | solution.py:296
  12.7 2.3 %collective-permute-start = (f32[32,32,128]{2,1,0:T(8,128)S(1)}, f32[32,32,128]{2,1,0:T(8,128)S(1)}, u32[]{:S(2)}, u32[]{:S(2)}) collective-permute-start(f32[32,32,128]{2,1,0:T(8,128)S(1)} %get-tuple-element.47), channel_id=1, source_target_pairs={{0,128},{4,132},{8,136},{12,140},{16,144},{20,148},{24,152},{28,15... | collective-permute-start | bytes 1572872 | tf_op jit(solution)/shard_map/cond/branch_0_fun/ppermute | solution.py:314
  15.0 1.2 %prepare.1 = (f32[28,16,128]{2,1,0:T(8,128)S(1)}, f32[28,16,128]{2,1,0:T(8,128)S(1)}, f32[28,16,128]{2,1,0:T(8,128)S(1)}) custom-call(s32[192]{0:T(256)S(1)} %get-tuple-element.50.ids, f32[28,16,128]{2,1,0:T(8,128)S(1)} %get-tuple-element.51.anchor, f32[28,16,128]{2,1,0:T(8,128)S(1)} %get-tuple-element.52.momentum), custom_call_target="tpu_custom_call" | custom-call | tf_op jit(solution)/shard_map/cond/branch_0_fun/prepare/pallas_call | solution.py:304
  16.2 6.0 %collective-permute-done = f32[32,32,128]{2,1,0:T(8,128)S(1)} collective-permute-done((f32[32,32,128]{2,1,0:T(8,128)S(1)}, f32[32,32,128]{2,1,0:T(8,128)S(1)}, u32[]{:S(2)}, u32[]{:S(2)}) %collective-permute-start) | collective-permute-done | bytes 524320 | tf_op jit(solution)/shard_map/cond/branch_0_fun/ppermute | solution.py:314
  22.1 0.1 pad_maximum_fusion
  22.2 29.3 %all_to_all.16.received = f32[32,2,32,128]{3,2,1,0:T(8,128)S(1)} all-to-all(f32[32,2,32,128]{3,2,1,0:T(8,128)S(1)} %pad_maximum_fusion), channel_id=1, replica_groups={{0,4,8,12,16,20,24,28,32,36,40,44,48,52,56,60,64,68,72,76,80,84,88,92,9..., dimensions={0} | all-to-all | bytes 2097152 | tf_op jit(solution)/shard_map/cond/branch_0_fun/all_to_all | solution.py:318
  51.6 1.6 %outer.2 = (f32[28,16,128]{2,1,0:T(8,128)}, f32[28,16,128]{2,1,0:T(8,128)}, f32[64,32,128]{2,1,0:T(8,128)S(1)}) custom-call(s32[192]{0:T(256)S(1)} %get-tuple-element.50.ids, f32[32,2,32,128]{3,2,1,0:T(8,128)S(1)} %all_to_all.16.received, f32[28,16,128]{2,1,0:T(8,128)S(1)} %get-tuple-element.51.anchor, f32[28,16,128]{2,1,0:T(8,128)S(1)} %get-tuple-element.57.refs_0_, ...), custom_call_target="tpu_custom_call" | custom-call | tf_op jit(solution)/shard_map/cond/branch_0_fun/outer/pallas_call | solution.py:251
  53.2 27.3 %all_to_all.17 = f32[64,32,128]{2,1,0:T(8,128)S(1)} all-to-all(f32[64,32,128]{2,1,0:T(8,128)S(1)} %get-tuple-element.60), channel_id=1, replica_groups=mesh['path'=64,'shard'=4] {'path'}, dimensions={0} | all-to-all | bytes 2097152 | tf_op jit(solution)/shard_map/cond/branch_0_fun/all_to_all | solution.py:263
  80.5 1.3 %place.1 = f32[2,64,2048]{2,1,0:T(8,128)} custom-call(f32[64,32,128]{2,1,0:T(8,128)S(1)} %get-tuple-element.96.received), custom_call_target="tpu_custom_call" | custom-call | tf_op jit(solution)/shard_map/place/pallas_call | solution.py:324
  (6 shorter events, 0.0 us)
Async XLA Ops:
  0.6 3.8 %copy-start.6 = (s32[64]{0:T(128)S(1)}, s32[64]{0:T(128)}, u32[]{:S(2)}) copy-start(s32[64]{0:T(128)} %param.19) | copy-start | bytes 772
  0.6 3.8 %copy-start.7 = (s32[64]{0:T(128)S(1)}, s32[64]{0:T(128)}, u32[]{:S(2)}) copy-start(s32[64]{0:T(128)} %param.18) | copy-start | bytes 772
  0.7 3.7 %copy-start.8 = (s32[64]{0:T(128)S(1)}, s32[64]{0:T(128)}, u32[]{:S(2)}) copy-start(s32[64]{0:T(128)} %param.17) | copy-start | bytes 772
  1.8 5.1 %copy-start.3 = (f32[1,2,64,2048]{3,2,1,0:T(8,128)S(1)}, f32[1,2,64,2048]{3,2,1,0:T(8,128)}, u32[]{:S(2)}) copy-start(f32[1,2,64,2048]{3,2,1,0:T(8,128)} %param.14) | copy-start | bytes 3145732
  1.8 5.1 %copy-start.4 = (f32[1,2,64,2048]{3,2,1,0:T(8,128)S(1)}, f32[1,2,64,2048]{3,2,1,0:T(8,128)}, u32[]{:S(2)}) copy-start(f32[1,2,64,2048]{3,2,1,0:T(8,128)} %param.13) | copy-start | bytes 3145732
  1.9 2.6 %collective-permute-start.1 = (f32[8,128]{1,0:T(8,128)S(1)}, f32[8,128]{1,0:T(8,128)S(1)}, u32[]{:S(2)}, u32[]{:S(2)}) collective-permute-start(f32[8,128]{1,0:T(8,128)S(1)} %norm.1), channel_id=1, source_target_pairs={{0,1},{1,0},{2,3},{3,2},{4,5},{5,4},{6,7},{7,6},{8,9},{9,8},{10,11... | collective-permute-start | bytes 12296 | tf_op jit(solution)/shard_map/ppermute | solution.py:237
  4.5 5.3 %copy-start = (bf16[1,2,64,2048]{3,2,1,0:T(8,128)(2,1)S(1)}, bf16[1,2,64,2048]{3,2,1,0:T(8,128)(2,1)}, u32[]{:S(2)}) copy-start(bf16[1,2,64,2048]{3,2,1,0:T(8,128)(2,1)} %param.12) | copy-start | bytes 1572868
  4.5 5.3 %copy-start.1 = (f32[2,64,2048]{2,1,0:T(8,128)S(1)}, f32[2,64,2048]{2,1,0:T(8,128)}, u32[]{:S(2)}) copy-start(f32[2,64,2048]{2,1,0:T(8,128)} %multiply_bitcast_fusion) | copy-start | bytes 3145732
  4.5 5.2 %copy-start.2 = (f32[28,1,2048]{2,1,0:T(1,128)S(1)}, f32[28,1,2048]{2,1,0:T(1,128)}, u32[]{:S(2)}) copy-start(f32[28,1,2048]{2,1,0:T(1,128)} %param.15) | copy-start | bytes 688132
  4.5 5.2 %copy-start.5 = (f32[28,1,2048]{2,1,0:T(1,128)S(1)}, f32[28,1,2048]{2,1,0:T(1,128)}, u32[]{:S(2)}) copy-start(f32[28,1,2048]{2,1,0:T(1,128)} %param.16) | copy-start | bytes 688132
  4.5 5.2 %collective-permute-start.2 = (f32[8,128]{1,0:T(8,128)S(1)}, f32[8,128]{1,0:T(8,128)S(1)}, u32[]{:S(2)}, u32[]{:S(2)}) collective-permute-start(f32[8,128]{1,0:T(8,128)S(1)} %add.3), channel_id=1, source_target_pairs={{0,2},{1,3},{2,0},{3,1},{4,6},{5,7},{6,4},{7,5},{8,10},{9,11},{10,... | collective-permute-start | bytes 12296 | tf_op jit(solution)/shard_map/ppermute | solution.py:241
  12.7 9.4 %collective-permute-start = (f32[32,32,128]{2,1,0:T(8,128)S(1)}, f32[32,32,128]{2,1,0:T(8,128)S(1)}, u32[]{:S(2)}, u32[]{:S(2)}) collective-permute-start(f32[32,32,128]{2,1,0:T(8,128)S(1)} %get-tuple-element.47), channel_id=1, source_target_pairs={{0,128},{4,132},{8,136},{12,140},{16,144},{20,148},{24,152},{28,15... | collective-permute-start | bytes 1572872 | tf_op jit(solution)/shard_map/cond/branch_0_fun/ppermute | solution.py:314
